TPU v7x, 32 devices: a whole 2x2x4 slice. The times are simulated.
32 devices in a mesh: dp: 8 (over z, y), mp: 4 (over x, core).
Axes of the slice: x: 2, y: 2, z: 4, core: 2. Of those that a mesh axis runs over, the one named last changes fastest.
Arguments:
- patches: bfloat16 [96, 196, 768], P(('dp', 'mp')), may hold values from -6 to 6
- partners: int32 [96], P(('dp', 'mp')), may hold values from 0 to 2
- mix_weight: float32 [96], P(('dp', 'mp')), may hold values from 0 to 1
- labels: int32 [96], P(('dp', 'mp')), may hold values from 0 to 999
- teacher_logits: float32 [96, 1000], P(('dp', 'mp')), may hold values from -60 to 60
- patch_weight: float32 [768, 384], P(('dp', 'mp')), may hold values from -0.21875 to 0.21875
- attn_weight: float32 [3, 384, 1536], P(None, None, ('dp', 'mp')), may hold values from -0.4082483 to 0.4082483
- mlp_weight: float32 [3, 2, 384, 1536], P(None, None, 'dp', 'mp'), may hold values from -0.3125 to 0.3125
- positions: float32 [198, 384], replicated, may hold values from -6 to 6
- head_weight: float32 [384, 2000], replicated, may hold values from -2 to 2
- norm_params: float32 [14, 384], replicated, may hold values from -1.2 to 1.4
- patch_first: float32 [768, 384], P(('dp', 'mp')), may hold values from -1.335144e-05 to 1.335144e-05
- attn_first: float32 [3, 384, 1536], P(None, None, ('dp', 'mp')), may hold values from -1.335144e-05 to 1.335144e-05
- mlp_first: float32 [3, 2, 384, 1536], P(None, None, 'dp', 'mp'), may hold values from -1.335144e-05 to 1.335144e-05
- pos_first: float32 [198, 384], replicated, may hold values from -1.335144e-05 to 1.335144e-05
- head_first: float32 [384, 2000], replicated, may hold values from -1.335144e-05 to 1.335144e-05
- norm_first: float32 [14, 384], replicated, may hold values from -1.335144e-05 to 1.335144e-05
- patch_second: float32 [768, 384], P(('dp', 'mp')), may hold values from 6.20512e-14 to 2.482048e-13
- attn_second: float32 [3, 384, 1536], P(None, None, ('dp', 'mp')), may hold values from 6.20512e-14 to 2.482048e-13
- mlp_second: float32 [3, 2, 384, 1536], P(None, None, 'dp', 'mp'), may hold values from 6.20512e-14 to 2.482048e-13
- pos_second: float32 [198, 384], replicated, may hold values from 6.20512e-14 to 2.482048e-13
- head_second: float32 [384, 2000], replicated, may hold values from 6.20512e-14 to 2.482048e-13
- norm_second: float32 [14, 384], replicated, may hold values from 6.20512e-14 to 2.482048e-13
Outputs:
- loss_sum: float32 [], replicated
- global_norm: float32 [], replicated
- new_patch: float32 [768, 384], P(('dp', 'mp'))
- new_attn: float32 [3, 384, 1536], P(None, None, ('dp', 'mp'))
- new_mlp: float32 [3, 2, 384, 1536], P(None, None, 'dp', 'mp')
- new_pos: float32 [198, 384], replicated
- new_head: float32 [384, 2000], replicated
- new_norms: float32 [14, 384], replicated
- patch_first_new: float32 [768, 384], P(('dp', 'mp'))
- attn_first_new: float32 [3, 384, 1536], P(None, None, ('dp', 'mp'))
- mlp_first_new: float32 [3, 2, 384, 1536], P(None, None, 'dp', 'mp')
- pos_first_new: float32 [198, 384], replicated
- head_first_new: float32 [384, 2000], replicated
- norm_first_new: float32 [14, 384], replicated
- patch_second_new: float32 [768, 384], P(('dp', 'mp'))
- attn_second_new: float32 [3, 384, 1536], P(None, None, ('dp', 'mp'))
- mlp_second_new: float32 [3, 2, 384, 1536], P(None, None, 'dp', 'mp')
- pos_second_new: float32 [198, 384], replicated
- head_second_new: float32 [384, 2000], replicated
- norm_second_new: float32 [14, 384], replicated
Inputs may be any that keep to these rules, and one draw needn't show every extreme that they name: `partners`: an image's partner is the image at this index among the 3 images of its aligned block.
All inputs are finite; a program needn't handle non-finite values.
Results may differ from a plain program's by a relative error of at most 0.025.
Values may be sent and summed in bfloat16 or wider, within the bound.
A program may use at most 256 MiB of HBM per device.

v0:
```python
import jax
import jax.numpy as jnp
from jax import lax
from jax.sharding import PartitionSpec as P

D = 384
HEADS = 6
C = 1000
PATCH_DIM = 768
NPATCH = 196
L = 3
HD = 64
TOK = 198


LN_EPS = 1e-06
TEMPER = 3.0
MAX_NORM = 0.02
BETA_ONE = 0.9
BETA_TWO = 0.999
STEP_RATES = (0.05, 0.05, 0.05, 0.4, 0.12, 0.5)
DECAY = 0.05
ADAM_EPS = 1e-08
ADAM_STEP = 10.0


def matmul(left_side, right_side):
    return jnp.dot(left_side, right_side, preferred_element_type=jnp.float32)


def matmul_tn(left_side, right_side):
    return lax.dot_general(
        left_side, right_side, (((0,), (0,)), ((), ())), preferred_element_type=jnp.float32
    )


def matmul_nt(left_side, right_side):
    return lax.dot_general(
        left_side, right_side, (((1,), (1,)), ((), ())), preferred_element_type=jnp.float32
    )


def gelu_exact(inputs):
    return jax.nn.gelu(inputs, approximate=False)


def norm_forward(inputs, norm_gain, norm_shift):
    centred = inputs - jnp.mean(inputs, axis=-1, keepdims=True)
    inverse = lax.rsqrt(jnp.mean(centred * centred, axis=-1, keepdims=True) + LN_EPS)
    normed = centred * inverse
    return (normed * norm_gain + norm_shift, normed, inverse)


def norm_backward(grad_out, normed, inverse, norm_gain):
    width = grad_out.shape[-1]
    grad_gain = jnp.sum((grad_out * normed).reshape(-1, width), axis=0)
    grad_shift = jnp.sum(grad_out.reshape(-1, width), axis=0)
    scaled = grad_out * norm_gain
    grad_in = inverse * (
        scaled
        - jnp.mean(scaled, axis=-1, keepdims=True)
        - normed * jnp.mean(scaled * normed, axis=-1, keepdims=True)
    )
    return (grad_in, grad_gain, grad_shift)


def score_block(queries, key_rows):
    return jnp.einsum(
        "bqhe,bkhe->bhqk", queries, key_rows, preferred_element_type=jnp.float32
    ) * HD ** (-0.5)


def layer_forward(stream, attn_layer, mlp_layer, norm_here):
    row_count = stream.shape[0]
    images = row_count // TOK
    normed_in, unit_a, inv_a = norm_forward(stream, norm_here[0], norm_here[1])
    act_a = normed_in.astype(jnp.bfloat16)
    proj_qkv = (
        matmul(act_a, attn_layer[:, : 3 * D])
        .astype(jnp.bfloat16)
        .reshape(images, TOK, 3, HEADS, HD)
    )
    scores = score_block(proj_qkv[:, :, 0], proj_qkv[:, :, 1])
    row_max = jnp.max(scores, axis=-1, keepdims=True)
    log_total = row_max + jnp.log(jnp.sum(jnp.exp(scores - row_max), axis=-1, keepdims=True))
    attn_probs = jnp.exp(scores - log_total).astype(jnp.bfloat16)
    attended = jnp.einsum(
        "bhqk,bkhe->bqhe", attn_probs, proj_qkv[:, :, 2], preferred_element_type=jnp.float32
    )
    attended = attended.astype(jnp.bfloat16).reshape(row_count, D)
    middle = stream + matmul(attended, attn_layer[:, 3 * D :])
    normed_mid, unit_b, inv_b = norm_forward(middle, norm_here[2], norm_here[3])
    act_b = normed_mid.astype(jnp.bfloat16)
    hidden = matmul(act_b, mlp_layer[0])
    gelu_low = gelu_exact(hidden).astype(jnp.bfloat16)
    branch_sum = matmul_nt(gelu_low, mlp_layer[1])
    saved = (
        unit_a,
        inv_a,
        act_a,
        proj_qkv,
        log_total,
        attended,
        unit_b,
        inv_b,
        act_b,
        hidden,
        gelu_low,
    )
    return (middle + branch_sum, saved)


def layer_backward(grad_in, attn_layer, mlp_layer, norm_here, saved):
    (
        unit_a,
        inv_a,
        act_a,
        proj_qkv,
        log_total,
        attended,
        unit_b,
        inv_b,
        group_rows,
        hidden,
        gelu_low,
    ) = saved
    row_count = grad_in.shape[0]
    images = row_count // TOK
    grad_low = grad_in.astype(jnp.bfloat16)
    grad_second = matmul_tn(grad_low, gelu_low)
    grad_gelu = matmul(grad_low, mlp_layer[1])
    grad_hidden = jax.vjp(gelu_exact, hidden)[1](grad_gelu)[0].astype(jnp.bfloat16)
    grad_first = matmul_tn(group_rows, grad_hidden)
    grad_act_b = matmul_nt(grad_hidden, mlp_layer[0])
    grad_norm_b, grad_g2, grad_b2 = norm_backward(grad_act_b, unit_b, inv_b, norm_here[2])
    grad_middle = grad_in + grad_norm_b
    grad_branch = grad_middle.astype(jnp.bfloat16)
    grad_out_proj = matmul_tn(attended, grad_branch)
    grad_attended = (
        matmul_nt(grad_branch, attn_layer[:, 3 * D :])
        .astype(jnp.bfloat16)
        .reshape(images, TOK, HEADS, HD)
    )
    queries = proj_qkv[:, :, 0]
    key_rows = proj_qkv[:, :, 1]
    values = proj_qkv[:, :, 2]
    attn_probs = jnp.exp(score_block(queries, key_rows) - log_total)
    grad_values = jnp.einsum(
        "bhqk,bqhe->bkhe",
        attn_probs.astype(jnp.bfloat16),
        grad_attended,
        preferred_element_type=jnp.float32,
    )
    grad_probs = jnp.einsum(
        "bqhe,bkhe->bhqk", grad_attended, values, preferred_element_type=jnp.float32
    )
    grad_scores = (
        attn_probs * (grad_probs - jnp.sum(grad_probs * attn_probs, axis=-1, keepdims=True))
    ).astype(jnp.bfloat16)
    grad_queries = jnp.einsum(
        "bhqk,bkhe->bqhe", grad_scores, key_rows, preferred_element_type=jnp.float32
    ) * HD ** (-0.5)
    grad_keys = jnp.einsum(
        "bhqk,bqhe->bkhe", grad_scores, queries, preferred_element_type=jnp.float32
    ) * HD ** (-0.5)
    grad_qkv = (
        jnp.stack([grad_queries, grad_keys, grad_values], axis=2)
        .astype(jnp.bfloat16)
        .reshape(row_count, 3 * D)
    )
    grad_proj = matmul_tn(act_a, grad_qkv)
    grad_act_a = matmul_nt(grad_qkv, attn_layer[:, : 3 * D])
    grad_norm_a, grad_g1, grad_b1 = norm_backward(grad_act_a, unit_a, inv_a, norm_here[0])
    grad_attn = jnp.concatenate([grad_proj, grad_out_proj], axis=1)
    return (
        grad_middle + grad_norm_a,
        grad_attn,
        jnp.stack([grad_first, grad_second]),
        jnp.stack([grad_g1, grad_b1, grad_g2, grad_b2]),
    )


def adam_update(weight, first_moment, second, grad_in, factor, step_rate):
    clipped = grad_in * factor
    first_moment = BETA_ONE * first_moment + (1.0 - BETA_ONE) * clipped
    second = BETA_TWO * second + (1.0 - BETA_TWO) * clipped * clipped
    adam_move = (
        first_moment
        / (1.0 - BETA_ONE**ADAM_STEP)
        / (jnp.sqrt(second / (1.0 - BETA_TWO**ADAM_STEP)) + ADAM_EPS)
    )
    return (weight - step_rate * (adam_move + DECAY * weight), first_moment, second)


def per_device(
    patches,
    partners,
    mix_weight,
    labels,
    teacher_logits,
    patch_weight,
    attn_weight,
    mlp_weight,
    positions,
    head_weight,
    norm_params,
    patch_first,
    attn_first,
    mlp_first,
    pos_first,
    head_first,
    norm_first,
    patch_second,
    attn_second,
    mlp_second,
    pos_second,
    head_second,
    norm_second,
):
    patch_low, attn_low = (
        lax.all_gather(patch_weight.astype(jnp.bfloat16), ("dp", "mp"), axis=0, tiled=True),
        lax.all_gather(attn_weight.astype(jnp.bfloat16), ("dp", "mp"), axis=2, tiled=True),
    )
    mlp_low = lax.all_gather(mlp_weight.astype(jnp.bfloat16), "dp", axis=2, tiled=True)
    mlp_low = lax.all_gather(mlp_low, "mp", axis=3, tiled=True)
    head_low = head_weight.astype(jnp.bfloat16)
    images = patches.shape[0]
    image_count = images * lax.axis_size("dp") * lax.axis_size("mp")
    own_rows = patches.astype(jnp.float32)
    partner_rows = jnp.take(patches, partners, axis=0).astype(jnp.float32)
    mix_rows = mix_weight[:, None, None]
    mixed_rows = (
        (mix_rows * own_rows + (1.0 - mix_rows) * partner_rows)
        .astype(jnp.bfloat16)
        .reshape(images * NPATCH, PATCH_DIM)
    )
    embedded = matmul(mixed_rows, patch_low).reshape(images, NPATCH, D) + positions[2:]
    lead_rows = jnp.broadcast_to(positions[:2], (images, 2, D))
    stream = jnp.concatenate([lead_rows, embedded], axis=1).reshape(images * TOK, D)
    saved_layers = []
    for depth_index in range(L):
        stream, saved = layer_forward(
            stream,
            attn_low[depth_index],
            mlp_low[depth_index],
            norm_params[4 * depth_index : 4 * depth_index + 4],
        )
        saved_layers.append(saved)
    final_in = stream.reshape(images, TOK, D)[:, :2]
    final_norm, unit_f, inv_f = norm_forward(final_in, norm_params[4 * L], norm_params[4 * L + 1])
    features = final_norm.astype(jnp.bfloat16)
    logits_cls = matmul(features[:, 0], head_low[:, :C])
    logits_dist = matmul(features[:, 1], head_low[:, C:])
    classes = lax.broadcasted_iota(jnp.int32, (images, C), 1)
    partner_labels = jnp.take(labels, partners, axis=0)
    target = mix_weight[:, None] * (classes == labels[:, None]).astype(jnp.float32) + (
        1.0 - mix_weight[:, None]
    ) * (classes == partner_labels[:, None]).astype(jnp.float32)
    log_cls = jax.nn.log_softmax(logits_cls, axis=-1)
    teacher_log = jax.nn.log_softmax(teacher_logits / TEMPER, axis=-1)
    student_log = jax.nn.log_softmax(logits_dist / TEMPER, axis=-1)
    teacher_prob = jnp.exp(teacher_log)
    per_image = 0.5 * -jnp.sum(target * log_cls, axis=-1) + 0.5 * TEMPER * TEMPER * jnp.sum(
        teacher_prob * (teacher_log - student_log), axis=-1
    )
    loss_part = jnp.sum(per_image)
    grad_cls = (0.5 / image_count * (jnp.exp(log_cls) - target)).astype(jnp.bfloat16)
    grad_dist = (0.5 * TEMPER / image_count * (jnp.exp(student_log) - teacher_prob)).astype(
        jnp.bfloat16
    )
    grad_head = jnp.concatenate(
        [matmul_tn(features[:, 0], grad_cls), matmul_tn(features[:, 1], grad_dist)], axis=1
    )
    grad_features = jnp.stack(
        [matmul_nt(grad_cls, head_low[:, :C]), matmul_nt(grad_dist, head_low[:, C:])], axis=1
    )
    grad_final, grad_gf, grad_bf = norm_backward(grad_features, unit_f, inv_f, norm_params[4 * L])
    grad_stream = (
        jnp.zeros((images, TOK, D), jnp.float32).at[:, :2].set(grad_final).reshape(images * TOK, D)
    )
    attn_grads = [None] * L
    mlp_grads = [None] * L
    norm_grads = [None] * L
    for depth_index in reversed(range(L)):
        grad_stream, attn_grads[depth_index], mlp_grads[depth_index], norm_grads[depth_index] = (
            layer_backward(
                grad_stream,
                attn_low[depth_index],
                mlp_low[depth_index],
                norm_params[4 * depth_index : 4 * depth_index + 4],
                saved_layers[depth_index],
            )
        )
    grad_embed = grad_stream.reshape(images, TOK, D)
    grad_pos = jnp.sum(grad_embed, axis=0)
    grad_patch = matmul_tn(
        mixed_rows, grad_embed[:, 2:].reshape(images * NPATCH, D).astype(jnp.bfloat16)
    )
    grad_norms = jnp.concatenate(norm_grads + [jnp.stack([grad_gf, grad_bf])], axis=0)
    grad_mlp = jnp.stack(mlp_grads)
    patch_share, attn_share = (
        lax.psum_scatter(grad_patch, ("dp", "mp"), scatter_dimension=0, tiled=True),
        lax.psum_scatter(jnp.stack(attn_grads), ("dp", "mp"), scatter_dimension=2, tiled=True),
    )
    grad_mlp = lax.psum_scatter(grad_mlp, "mp", scatter_dimension=3, tiled=True)
    mlp_share = lax.psum_scatter(grad_mlp, "dp", scatter_dimension=2, tiled=True)
    pos_sum, head_sum, norm_sum, loss_sum = lax.psum(
        (grad_pos, grad_head, grad_norms, loss_part), ("dp", "mp")
    )
    own_squares = (
        jnp.sum(patch_share * patch_share)
        + jnp.sum(attn_share * attn_share)
        + jnp.sum(mlp_share * mlp_share)
    )
    shared = (
        jnp.sum(pos_sum * pos_sum) + jnp.sum(head_sum * head_sum) + jnp.sum(norm_sum * norm_sum)
    )
    global_norm = jnp.sqrt(lax.psum(own_squares, ("dp", "mp")) + shared)
    factor = jnp.minimum(1.0, MAX_NORM / global_norm)
    new_patch, patch_m, patch_v = adam_update(
        patch_weight, patch_first, patch_second, patch_share, factor, STEP_RATES[0]
    )
    new_attn, attn_m, attn_v = adam_update(
        attn_weight, attn_first, attn_second, attn_share, factor, STEP_RATES[1]
    )
    new_mlp, mlp_m, mlp_v = adam_update(
        mlp_weight, mlp_first, mlp_second, mlp_share, factor, STEP_RATES[2]
    )
    new_pos, pos_m, pos_v = adam_update(
        positions, pos_first, pos_second, pos_sum, factor, STEP_RATES[3]
    )
    new_head, head_m, head_v = adam_update(
        head_weight, head_first, head_second, head_sum, factor, STEP_RATES[4]
    )
    new_norms, norms_m, norms_v = adam_update(
        norm_params, norm_first, norm_second, norm_sum, factor, STEP_RATES[5]
    )
    return (
        loss_sum,
        global_norm,
        new_patch,
        new_attn,
        new_mlp,
        new_pos,
        new_head,
        new_norms,
        patch_m,
        attn_m,
        mlp_m,
        pos_m,
        head_m,
        norms_m,
        patch_v,
        attn_v,
        mlp_v,
        pos_v,
        head_v,
        norms_v,
    )


def solution(mesh):
    placed = (
        P(("dp", "mp"), None, None),
        P(("dp", "mp")),
        P(("dp", "mp")),
        P(("dp", "mp")),
        P(("dp", "mp"), None),
        P(("dp", "mp"), None),
        P(None, None, ("dp", "mp")),
        P(None, None, "dp", "mp"),
        P(),
        P(),
        P(),
        P(("dp", "mp"), None),
        P(None, None, ("dp", "mp")),
        P(None, None, "dp", "mp"),
        P(),
        P(),
        P(),
        P(("dp", "mp"), None),
        P(None, None, ("dp", "mp")),
        P(None, None, "dp", "mp"),
        P(),
        P(),
        P(),
    )
    return jax.shard_map(
        per_device,
        mesh=mesh,
        in_specs=placed,
        out_specs=(
            P(),
            P(),
            P(("dp", "mp"), None),
            P(None, None, ("dp", "mp")),
            P(None, None, "dp", "mp"),
            P(),
            P(),
            P(),
            P(("dp", "mp"), None),
            P(None, None, ("dp", "mp")),
            P(None, None, "dp", "mp"),
            P(),
            P(),
            P(),
            P(("dp", "mp"), None),
            P(None, None, ("dp", "mp")),
            P(None, None, "dp", "mp"),
            P(),
            P(),
            P(),
        ),
        check_vma=False,
    )
```

profile of v0, /device:TPU:1, one launch (start us, length us, event | category | flops | bytes accessed | tf_op | source)
XLA Modules:
  0.0 974.8 jit_solution(14893067132696004443)
XLA Ops:
  10.9 47.8 %all-gather.6.cloned.1.call-done = bf16[3,2,384,384]{3,2,1,0:T(8,128)(2,1)} async-done(((bf16[3,2,48,384]{3,2,1,0:T(8,128)(2,1)}), bf16[3,2,384,384]{3,2,1,0:T(8,128)(2,1)}) %all-gather.6.cloned.1.call-update) | async-done | bytes 1769488 | tf_op jit(solution)/shard_map/all_gather | solution.py:224
  64.1 42.8 %all_gather.12 = bf16[768,384]{1,0:T(8,128)(2,1)S(1)} all-gather(bf16[24,384]{1,0:T(8,128)(2,1)S(1)} %convert_element_type.188), channel_id=1, replica_groups=mesh['dp'=8,'mp'=4] {'dp','mp'}, dimensions={0}, use_global_device_ids=true | all-gather | bytes 608256 | tf_op jit(solution)/shard_map/all_gather | solution.py:221
  111.3 11.8 %all-gather.4.cloned.1.call-done = bf16[3,384,1536]{1,2,0:T(8,128)(2,1)} async-done(((bf16[3,384,48]{1,2,0:T(8,128)(2,1)}), bf16[3,384,1536]{1,2,0:T(8,128)(2,1)}) %all-gather.4.cloned.1.call-update) | async-done | bytes 3538960 | tf_op jit(solution)/shard_map/all_gather | solution.py:222
  123.1 3.8 slice_bitcast_fusion.2
  129.0 3.9 reshape.496
  132.9 5.0 fusion.150
  148.7 25.5 %all-gather.8.cloned.1.call-done = bf16[3,2,384,1536]{3,2,1,0:T(8,128)(2,1)} async-done(((bf16[3,2,384,384]{3,2,1,0:T(8,128)(2,1)}), bf16[3,2,384,1536]{3,2,1,0:T(8,128)(2,1)}) %all-gather.8.cloned.1.call-update) | async-done | bytes 7077904 | tf_op jit(solution)/shard_map/all_gather | solution.py:225
  174.3 11.8 %multiply_convert_fusion.5 = (bf16[594,1536]{1,0:T(8,128)(2,1)S(1)}, f32[594,1536]{1,0:T(8,128)}, f32[594,1536]{1,0:T(8,128)}) fusion(bf16[3,2,384,1536]{3,2,1,0:T(8,128)(2,1)} %all-gather.8.cloned.1.call-done, f32[594,384]{1,0:T(8,128)S(1)} %get-tuple-element.187, f32[384]{0:T(512)S(1)} %get-tuple-element.128, f32[384]{0:T(512)S(1)} %get-tuple-element.129, ...), kind=kOutput, calls=%fused_computation.53 | convolution fusion | flops 761156352 | bytes 11223696 | tf_op jit(solution)/shard_map/dot_general | solution.py:28
  186.1 3.2 fusion.153
  190.7 3.9 reshape.497
  194.5 4.1 fusion.149
  209.2 12.0 %multiply_convert_fusion.4 = (bf16[594,1536]{1,0:T(8,128)(2,1)S(1)}, f32[594,1536]{1,0:T(8,128)}, f32[594,1536]{1,0:T(8,128)}) fusion(bf16[3,2,384,1536]{3,2,1,0:T(8,128)(2,1)} %all-gather.8.cloned.1.call-done, f32[594,384]{1,0:T(8,128)S(1)} %get-tuple-element.194, f32[384]{0:T(512)S(1)} %get-tuple-element.124, f32[384]{0:T(512)S(1)} %get-tuple-element.125, ...), kind=kOutput, calls=%fused_computation.38 | convolution fusion | flops 761156352 | bytes 11223696 | tf_op jit(solution)/shard_map/dot_general | solution.py:28
  221.2 3.2 fusion.155
  225.8 3.8 reshape.498
  229.6 4.1 fusion.148
  244.6 11.8 %multiply_convert_fusion.3 = (bf16[594,1536]{1,0:T(8,128)(2,1)S(1)}, f32[594,1536]{1,0:T(8,128)}, f32[594,1536]{1,0:T(8,128)}) fusion(bf16[3,2,384,1536]{3,2,1,0:T(8,128)(2,1)} %all-gather.8.cloned.1.call-done, f32[594,384]{1,0:T(8,128)S(1)} %get-tuple-element.201, f32[384]{0:T(512)S(1)} %get-tuple-element.121, f32[384]{0:T(512)S(1)} %get-tuple-element.119, ...), kind=kOutput, calls=%fused_computation.23 | convolution fusion | flops 761156352 | bytes 11223696 | tf_op jit(solution)/shard_map/dot_general | solution.py:28
  257.6 3.5 convolution_add_fusion.1
  267.7 5.7 add_convert_fusion.2
  273.4 3.8 multiply_reduce_fusion.7
  281.2 3.0 fusion.35
  292.3 3.8 multiply_reduce_fusion.8
  296.7 3.3 add_convert_fusion.1
  300.1 3.9 multiply_reduce_fusion.9
  307.5 3.0 copy.257
  310.6 3.2 fusion.36
  325.8 2.7 convolution_bitcast_fusion.3
  328.9 3.0 copy.262
  331.8 5.6 convert_element_type.228
  337.5 3.5 multiply_reduce_fusion.10
  344.5 3.3 add_convert_fusion
  351.5 2.7 maximum_bitcast_fusion.2
  360.5 12.9 %pad_maximum_fusion = f32[3,2,384,1536]{3,2,1,0:T(8,128)} fusion(f32[1,2,384,1536]{3,2,1,0:T(8,128)} %maximum_bitcast_fusion.2, f32[1,2,384,1536]{3,2,1,0:T(8,128)} %maximum_bitcast_fusion.1, f32[1,2,384,1536]{3,2,1,0:T(8,128)} %maximum_bitcast_fusion), kind=kLoop, calls=%fused_computation.2 | loop fusion | flops 7077888 | bytes 28311552 | tf_op jit(solution)/shard_map/stack | solution.py:300
  375.3 3.9 multiply_reduce_fusion.11
  381.9 2.7 reshape.501
  387.2 4.5 multiply_reduce_fusion
  396.1 3.0 copy.269
  399.0 5.8 convert_element_type.235
  404.9 3.8 multiply_reduce_fusion.12
  422.6 2.8 convolution_bitcast_fusion.6
  433.5 3.5 pad_maximum_fusion.1
  437.1 10.8 %copy.273 = f32[3,384,1536]{1,0,2:T(4,128)} copy(f32[3,384,1536]{2,1,0:T(8,128)} %pad_maximum_fusion.1) | data formatting | bytes 14155776 | tf_op jit(solution)/shard_map/stack | solution.py:303
  451.9 30.8 %reduce-scatter.6.cloned.1.call-done = f32[3,2,384,384]{3,2,1,0:T(8,128)} async-done(((f32[3,2,384,1536]{3,2,1,0:T(8,128)}), f32[3,2,384,384]{3,2,1,0:T(8,128)}) %reduce-scatter.6.cloned.1.call-update) | async-done | bytes 3538960 | tf_op jit(solution)/shard_map/reduce_scatter | solution.py:305
  484.6 97.6 %reduce-scatter.10.cloned.1.call-done = f32[24,384]{1,0:T(8,128)} async-done(((f32[768,384]{1,0:T(8,128)}), f32[24,384]{1,0:T(8,128)}) %reduce-scatter.10.cloned.1.call-update) | async-done | bytes 36880
  583.6 240.6 %all-reduce.7.cloned.1.call-done = (f32[3,384,1536]{1,0,2:T(4,128)}, f32[198,384]{1,0:T(8,128)}, f32[384,2000]{0,1:T(8,128)}) async-done(((f32[3,384,1536]{1,0,2:T(4,128)}, f32[198,384]{1,0:T(8,128)}, f32[384,2000]{0,1:T(8,128)}), (f32[3,384,1536]{1,0,2:T(4,128)}, f32[198,384]{1,0:T(8,128)}, f32[384,2000]{0,1:T(8,128)})) %all-reduce.7.cloned.1.call-update) | async-done | bytes 10454032
  829.7 3.3 multiply_reduce_fusion.6
  832.9 74.2 %reduce-scatter.8.cloned.1.call-done = f32[3,2,48,384]{3,2,1,0:T(8,128)} async-done(((f32[3,2,384,384]{3,2,1,0:T(8,128)}), f32[3,2,48,384]{3,2,1,0:T(8,128)}) %reduce-scatter.8.cloned.1.call-update) | async-done | bytes 442384 | tf_op jit(solution)/shard_map/reduce_scatter | solution.py:306
  910.8 40.7 %all-reduce.3 = (f32[]{:T(128)}, f32[]{:T(128)}, f32[14,384]{1,0:T(8,128)S(1)}) all-reduce(f32[]{:T(128)} %add_reduce_fusion, f32[]{:T(128)S(6)} %add.401, f32[14,384]{1,0:T(8,128)S(1)} %concatenate.25), channel_id=1, replica_groups=mesh['dp'=8,'mp'=4] {'dp','mp'}, use_global_device_ids=true, to_apply=%region_25.27 | all-reduce | flops 5378 | bytes 43024 | tf_op jit(solution)/shard_map/psum | solution.py:307
  955.9 6.8 multiply_subtract_fusion
  (539 shorter events, 151.8 us)
Async XLA Ops:
  7.2 52.6 %copy-start.8 = (f32[384,2000]{0,1:T(8,128)S(1)}, f32[384,2000]{0,1:T(8,128)}, u32[]{:S(2)}) copy-start(f32[384,2000]{0,1:T(8,128)} %param.35) | copy-start | bytes 9216004
  7.2 51.5 %all-gather.6.cloned.1.call-start = ((), (), s32[]{:S(2)}) async-start(), calls=%async_computation.4 | async-start | bytes 1990656 | tf_op jit(solution)/shard_map/all_gather | solution.py:224
  9.1 51.9 %copy-start.99 = (f32[24,384]{1,0:T(8,128)S(1)}, f32[24,384]{1,0:T(8,128)}, u32[]{:S(2)}) copy-start(f32[24,384]{1,0:T(8,128)} %param.31) | copy-start | bytes 110596
  9.2 51.9 %copy-start.155 = (s32[3]{0:T(128)S(1)}, s32[3]{0:T(128)}, u32[]{:S(2)}) copy-start(s32[3]{0:T(128)} %param.27) | copy-start | bytes 40
  9.2 113.9 %all-gather.4.cloned.1.call-start = ((), (), s32[]{:S(2)}) async-start(), calls=%async_computation.3 | async-start | bytes 3649536 | tf_op jit(solution)/shard_map/all_gather | solution.py:222
  10.8 163.4 %all-gather.8.cloned.1.call-start = ((), (), s32[]{:S(2)}) async-start(), calls=%async_computation.5 | async-start | bytes 8847360 | tf_op jit(solution)/shard_map/all_gather | solution.py:225
  58.7 423.9 %reduce-scatter.6.cloned.1.call-start = ((), (), s32[]{:S(2)}) async-start(), calls=%async_computation.6 | async-start | bytes 17694720 | tf_op jit(solution)/shard_map/reduce_scatter | solution.py:305
  61.1 47.8 %slice-start = ((f32[198,384]{1,0:T(8,128)}), f32[2,384]{1,0:T(2,128)S(1)}, s32[]{:S(2)}) async-start(f32[198,384]{1,0:T(8,128)} %param.34), calls=%async_computation.10 | async-start | bytes 6144 | tf_op jit(solution)/shard_map/slice | solution.py:238
  62.9 46.7 %copy-start.84 = (bf16[3,196,768]{2,1,0:T(8,128)(2,1)}, bf16[3,196,768]{2,1,0:T(8,128)(2,1)S(1)}, u32[]{:S(2)}) copy-start(bf16[3,196,768]{2,1,0:T(8,128)(2,1)S(1)} %gather_fusion.1) | copy-start | bytes 2709508
  64.1 44.8 %copy-start.156 = (pred[3]{0:T(512)(128)(4,1)}, pred[3]{0:T(512)(128)(4,1)S(1)}, u32[]{:S(2)}) copy-start(pred[3]{0:T(512)(128)(4,1)S(1)} %get-tuple-element.161) | copy-start | bytes 13
  64.1 200.9 %copy-start.121 = (s32[3]{0:T(128)}, s32[3]{0:T(128)S(1)}, u32[]{:S(2)}) copy-start(s32[3]{0:T(128)S(1)} %get-tuple-element.160) | copy-start | bytes 40
  64.1 45.6 %copy-start.102 = (f32[14,384]{1,0:T(8,128)S(1)}, f32[14,384]{1,0:T(8,128)}, u32[]{:S(2)}) copy-start(f32[14,384]{1,0:T(8,128)} %param.36) | copy-start | bytes 64516
  109.2 17.7 %copy-start.112 = (f32[594]{0:T(1024)}, f32[594]{0:T(1024)S(1)}, u32[]{:S(2)}) copy-start(f32[594]{0:T(1024)S(1)} %div.186) | copy-start | bytes 7132
  109.7 17.2 %copy-start.114 = (f32[594]{0:T(1024)}, f32[594]{0:T(1024)S(1)}, u32[]{:S(2)}) copy-start(f32[594]{0:T(1024)S(1)} %rsqrt.61) | copy-start | bytes 7132
  109.8 17.1 %copy-start.110 = (f32[384]{0:T(512)}, f32[384]{0:T(512)S(1)}, u32[]{:S(2)}) copy-start(f32[384]{0:T(512)S(1)} %get-tuple-element.131) | copy-start | bytes 4612
  109.8 64.5 %copy-start.137 = (f32[384]{0:T(512)}, f32[384]{0:T(512)S(1)}, u32[]{:S(2)}) copy-start(f32[384]{0:T(512)S(1)} %get-tuple-element.128) | copy-start | bytes 4612
  109.8 79.8 %copy-start.131 = (f32[384]{0:T(512)}, f32[384]{0:T(512)S(1)}, u32[]{:S(2)}) copy-start(f32[384]{0:T(512)S(1)} %get-tuple-element.126) | copy-start | bytes 4612
  109.8 99.4 %copy-start.139 = (f32[384]{0:T(512)}, f32[384]{0:T(512)S(1)}, u32[]{:S(2)}) copy-start(f32[384]{0:T(512)S(1)} %get-tuple-element.124) | copy-start | bytes 4612
  109.8 114.9 %copy-start.133 = (f32[384]{0:T(512)}, f32[384]{0:T(512)S(1)}, u32[]{:S(2)}) copy-start(f32[384]{0:T(512)S(1)} %get-tuple-element.122) | copy-start | bytes 4612
  109.9 134.7 %copy-start.141 = (f32[384]{0:T(512)}, f32[384]{0:T(512)S(1)}, u32[]{:S(2)}) copy-start(f32[384]{0:T(512)S(1)} %get-tuple-element.121) | copy-start | bytes 4612
  111.0 35.6 %copy-start.11 = (f32[594,384]{1,0:T(8,128)}, f32[594,384]{1,0:T(8,128)S(1)}, u32[]{:S(2)}) copy-start(f32[594,384]{1,0:T(8,128)S(1)} %reshape.463) | copy-start | bytes 2737156
  111.3 152.8 %copy-start.125 = (f32[3]{0:T(128)}, f32[3]{0:T(128)S(1)}, u32[]{:S(2)}) copy-start(f32[3]{0:T(128)S(1)} %log.38) | copy-start | bytes 40
  146.7 39.4 %copy-start.55 = (bf16[594,384]{0,1:T(8,128)(2,1)}, bf16[594,384]{0,1:T(8,128)(2,1)S(1)}, u32[]{:S(2)}) copy-start(bf16[594,384]{0,1:T(8,128)(2,1)S(1)} %reshape.465) | copy-start | bytes 1368580
  148.4 37.7 %copy-start.19 = (f32[594,384]{1,0:T(8,128)}, f32[594,384]{1,0:T(8,128)S(1)}, u32[]{:S(2)}) copy-start(f32[594,384]{1,0:T(8,128)S(1)} %get-tuple-element.187) | copy-start | bytes 2737156
  189.3 17.8 %copy-start.13 = (f32[594,384]{1,0:T(8,128)}, f32[594,384]{1,0:T(8,128)S(1)}, u32[]{:S(2)}) copy-start(f32[594,384]{1,0:T(8,128)S(1)} %get-tuple-element.190) | copy-start | bytes 2737156
  207.1 14.1 %copy-start.57 = (bf16[594,384]{0,1:T(8,128)(2,1)}, bf16[594,384]{0,1:T(8,128)(2,1)S(1)}, u32[]{:S(2)}) copy-start(bf16[594,384]{0,1:T(8,128)(2,1)S(1)} %reshape.467) | copy-start | bytes 1368580
  224.4 18.1 %copy-start.16 = (f32[594,384]{1,0:T(8,128)}, f32[594,384]{1,0:T(8,128)S(1)}, u32[]{:S(2)}) copy-start(f32[594,384]{1,0:T(8,128)S(1)} %get-tuple-element.197) | copy-start | bytes 2737156
  244.3 33.0 %copy-start.24 = (f32[594,384]{1,0:T(8,128)}, f32[594,384]{1,0:T(8,128)S(1)}, u32[]{:S(2)}) copy-start(f32[594,384]{1,0:T(8,128)S(1)} %get-tuple-element.201) | copy-start | bytes 2737156
  373.4 208.8 %reduce-scatter.10.cloned.1.call-start = ((), (), s32[]{:S(2)}) async-start(), calls=%async_computation.8 | async-start | bytes 1216512
  430.4 393.8 %all-reduce.7.cloned.1.call-start = ((), (), s32[]{:S(2)}) async-start(), calls=%async_computation.9 | async-start | bytes 25632768
  451.6 31.0 %copy-start.154 = (f32[384]{0:T(512)S(1)}, f32[384]{0:T(512)}, u32[]{:S(2)}) copy-start(f32[384]{0:T(512)} %get-tuple-element.103) | copy-start | bytes 4612
  451.7 31.0 %copy-start.153 = (f32[384]{0:T(512)S(1)}, f32[384]{0:T(512)}, u32[]{:S(2)}) copy-start(f32[384]{0:T(512)} %get-tuple-element.118) | copy-start | bytes 4612
  451.7 31.1 %copy-start.152 = (f32[384]{0:T(512)S(1)}, f32[384]{0:T(512)}, u32[]{:S(2)}) copy-start(f32[384]{0:T(512)} %get-tuple-element.101) | copy-start | bytes 4612
  451.7 31.1 %copy-start.151 = (f32[384]{0:T(512)S(1)}, f32[384]{0:T(512)}, u32[]{:S(2)}) copy-start(f32[384]{0:T(512)} %get-tuple-element.117) | copy-start | bytes 4612
  451.7 31.1 %copy-start.150 = (f32[384]{0:T(512)S(1)}, f32[384]{0:T(512)}, u32[]{:S(2)}) copy-start(f32[384]{0:T(512)} %get-tuple-element.99) | copy-start | bytes 4612
  451.7 31.1 %copy-start.149 = (f32[384]{0:T(512)S(1)}, f32[384]{0:T(512)}, u32[]{:S(2)}) copy-start(f32[384]{0:T(512)} %get-tuple-element.116) | copy-start | bytes 4612
  451.7 31.1 %copy-start.148 = (f32[384]{0:T(512)S(1)}, f32[384]{0:T(512)}, u32[]{:S(2)}) copy-start(f32[384]{0:T(512)} %get-tuple-element.97) | copy-start | bytes 4612
  451.7 31.1 %copy-start.147 = (f32[384]{0:T(512)S(1)}, f32[384]{0:T(512)}, u32[]{:S(2)}) copy-start(f32[384]{0:T(512)} %get-tuple-element.115) | copy-start | bytes 4612
  451.7 31.1 %copy-start.146 = (f32[384]{0:T(512)S(1)}, f32[384]{0:T(512)}, u32[]{:S(2)}) copy-start(f32[384]{0:T(512)} %get-tuple-element.95) | copy-start | bytes 4612
  451.7 31.2 %copy-start.145 = (f32[384]{0:T(512)S(1)}, f32[384]{0:T(512)}, u32[]{:S(2)}) copy-start(f32[384]{0:T(512)} %get-tuple-element.114) | copy-start | bytes 4612
  451.7 31.2 %copy-start.144 = (f32[384]{0:T(512)S(1)}, f32[384]{0:T(512)}, u32[]{:S(2)}) copy-start(f32[384]{0:T(512)} %get-tuple-element.93) | copy-start | bytes 4612
  451.7 31.2 %copy-start.143 = (f32[384]{0:T(512)S(1)}, f32[384]{0:T(512)}, u32[]{:S(2)}) copy-start(f32[384]{0:T(512)} %get-tuple-element.113) | copy-start | bytes 4612
  451.8 31.2 %copy-start.116 = (f32[384]{0:T(512)S(1)}, f32[384]{0:T(512)}, u32[]{:S(2)}) copy-start(f32[384]{0:T(512)} %get-tuple-element.105) | copy-start | bytes 4612
  451.8 31.2 %copy-start.135 = (f32[384]{0:T(512)S(1)}, f32[384]{0:T(512)}, u32[]{:S(2)}) copy-start(f32[384]{0:T(512)} %get-tuple-element.221) | copy-start | bytes 4612
  451.8 31.2 %copy-start.136 = (f32[384]{0:T(512)S(1)}, f32[384]{0:T(512)}, u32[]{:S(2)}) copy-start(f32[384]{0:T(512)} %get-tuple-element.219) | copy-start | bytes 4612
  451.8 455.3 %reduce-scatter.8.cloned.1.call-start = ((), (), s32[]{:S(2)}) async-start(), calls=%async_computation.7 | async-start | bytes 3981312 | tf_op jit(solution)/shard_map/reduce_scatter | solution.py:306
  482.6 470.8 %copy-start.81 = (f32[198,384]{1,0:T(8,128)S(1)}, f32[198,384]{1,0:T(8,128)}, u32[]{:S(2)}) copy-start(f32[198,384]{1,0:T(8,128)} %param.34) | copy-start | bytes 912388
  824.2 131.5 %copy-start.7 = (f32[384,2000]{0,1:T(8,128)S(1)}, f32[384,2000]{0,1:T(8,128)}, u32[]{:S(2)}) copy-start(f32[384,2000]{0,1:T(8,128)} %get-tuple-element.139) | copy-start | bytes 9216004
  (127 other events, 663.0 us)
Sparse Core Ops, SparseCore 0:
  10.8 47.7 all-gather.5
  62.2 60.8 all-gather.3
  124.7 49.5 all-gather.7
  373.5 109.0 reduce-scatter.5
  487.6 94.5 reduce-scatter.9
  589.0 235.1 all-reduce.6
  828.3 78.8 reduce-scatter.7
where the time goes:
time: 984 us; the launch traced here: 975 us
  waiting for transfers between devices  528 us (54%)
  matrix products  152 us (15%)
  local copies, waits for them, and re-layouts  112 us (11%)
  blocking collectives  83.5 us (8%)
  other arithmetic  75.7 us (8%)
  between operations  22.9 us (2%)
    unnamed x9, waiting for transfers between devices  338 us
    reduce_scatter x1, waiting for transfers between devices, per_device(): lax.psum_scatter(grad_mlp, 'dp', scatter_dimension=2, tiled=True)  74.2 us
    dot_general x15, matrix products, matmul(): return jnp.dot(left_side, right_side, preferred_element_type=jnp.float32)  59 us
    all_gather x1, waiting for transfers between devices, per_device(): lax.all_gather(mlp_weight.astype(jnp.bfloat16), 'dp', axis=2, tiled=True)  47.8 us
    all_gather x1, blocking collectives, per_device(): lax.all_gather(patch_weight.astype(jnp.bfloat16), ('dp', 'mp'), axis=0, t...  42.8 us
    psum x1, blocking collectives, per_device(): lax.psum((grad_pos, grad_head, grad_norms, loss_part), ('dp', 'mp'))  40.7 us
    dot_general x14, matrix products, matmul_nt(): lax.dot_general(left_side, right_side, (((1,), (1,)), ((), ())), preferre...  40.1 us
    reduce_scatter x1, waiting for transfers between devices, per_device(): grad_mlp = lax.psum_scatter(grad_mlp, 'mp', scatter_dimension=3, tiled=True)  30.8 us
  transfers between devices with their start and end apart: 7, of which 7 were waited for; matrix products, arithmetic and copies ran while one was open for 12% of the time, Pallas kernels for 0%

commit v1 on v0

v1 whole, which is shorter than its diff:
```python
import jax
import jax.numpy as jnp
from jax import lax
from jax.experimental import pallas as pl
from jax.experimental.pallas import tpu as pltpu
from jax.sharding import PartitionSpec as P

D = 384
C = 1000
PATCH_DIM = 768
NPATCH = 196
L = 3
TOK = 198
IMG = 3
ROWS = 208
ALL = IMG * ROWS
BLOCKS = 4

LN_EPS = 1e-06
TEMPER = 3.0
MAX_NORM = 0.02
BETA_ONE = 0.9
BETA_TWO = 0.999
STEP_RATES = (0.05, 0.05, 0.05, 0.4, 0.12, 0.5)
DECAY = 0.05
ADAM_EPS = 1e-08
ADAM_STEP = 10.0
LOWEST = -1e30

BF16 = jnp.bfloat16
F32 = jnp.float32
VMEM = pl.BlockSpec(memory_space=pltpu.VMEM)
SMEM = pl.BlockSpec(memory_space=pltpu.SMEM)
HBM = pl.BlockSpec(memory_space=pl.ANY)


def nn(left, right):
    return jnp.dot(left, right, preferred_element_type=F32)


def nt(left, right):
    return lax.dot_general(left, right, (((1,), (1,)), ((), ())), preferred_element_type=F32)


def tn(left, right):
    return lax.dot_general(left, right, (((0,), (0,)), ((), ())), preferred_element_type=F32)


def unit_norm(inputs):
    centred = inputs - jnp.mean(inputs, axis=-1, keepdims=True)
    inverse = lax.rsqrt(jnp.mean(centred * centred, axis=-1, keepdims=True) + LN_EPS)
    return centred * inverse, inverse


def norm_backward(grad_out, inputs, gain):
    normed, inverse = unit_norm(inputs)
    grad_gain = jnp.sum(grad_out * normed, axis=0, keepdims=True)
    grad_shift = jnp.sum(grad_out, axis=0, keepdims=True)
    scaled = grad_out * gain
    grad_in = inverse * (
        scaled
        - jnp.mean(scaled, axis=-1, keepdims=True)
        - normed * jnp.mean(scaled * normed, axis=-1, keepdims=True)
    )
    return grad_in, grad_gain, grad_shift


def head_lanes(shape, head):
    lane = lax.broadcasted_iota(jnp.int32, shape, len(shape) - 1)
    return lane < 64 if head == 0 else lane >= 64


def attend(qkv, out, image, pair):
    rows = slice(image * ROWS, (image + 1) * ROWS)
    lanes = 128 * pair
    queries = qkv[rows, lanes : lanes + 128] * BF16(0.125)
    keys = qkv[rows, D + lanes : D + lanes + 128]
    values = qkv[rows, 2 * D + lanes : 2 * D + lanes + 128]
    key_lane = lax.broadcasted_iota(jnp.int32, (1, ROWS), 1)
    parts = []
    for head in range(2):
        scores = nt(jnp.where(head_lanes((ROWS, 128), head), queries, BF16(0)), keys)
        scores = jnp.where(key_lane < TOK, scores, LOWEST)
        weights = jnp.exp(scores - jnp.max(scores, axis=-1, keepdims=True))
        inverse = 1.0 / jnp.sum(weights, axis=-1, keepdims=True)
        parts.append(nn(weights.astype(BF16), values) * inverse)
    out[rows, lanes : lanes + 128] = jnp.where(
        head_lanes((ROWS, 128), 0), parts[0], parts[1]
    ).astype(BF16)


def attend_backward(qkv, grad_out, grad_qkv, image, pair):
    rows = slice(image * ROWS, (image + 1) * ROWS)
    lanes = 128 * pair
    queries = qkv[rows, lanes : lanes + 128] * BF16(0.125)
    keys = qkv[rows, D + lanes : D + lanes + 128]
    values = qkv[rows, 2 * D + lanes : 2 * D + lanes + 128]
    grad = grad_out[rows, lanes : lanes + 128]
    key_row = lax.broadcasted_iota(jnp.int32, (ROWS, 1), 0)
    grad_q, grad_k, grad_v = [], [], []
    for head in range(2):
        own = head_lanes((ROWS, 128), head)
        scores = nt(jnp.where(own, keys, BF16(0)), queries)
        scores = jnp.where(key_row < TOK, scores, LOWEST)
        probs = jnp.exp(scores - jnp.max(scores, axis=0, keepdims=True))
        probs = probs * (1.0 / jnp.sum(probs, axis=0, keepdims=True))
        grad_probs = nt(jnp.where(own, values, BF16(0)), grad)
        total = jnp.sum(probs * grad_probs, axis=0, keepdims=True)
        grad_scores = (probs * (grad_probs - total)).astype(BF16)
        grad_v.append(nn(probs.astype(BF16), grad))
        grad_k.append(nn(grad_scores, queries))
        grad_q.append(tn(grad_scores, keys))
    first = head_lanes((ROWS, 128), 0)
    grad_qkv[rows, lanes : lanes + 128] = (
        jnp.where(first, grad_q[0], grad_q[1]) * 0.125
    ).astype(BF16)
    grad_qkv[rows, D + lanes : D + lanes + 128] = jnp.where(first, grad_k[0], grad_k[1]).astype(
        BF16
    )
    grad_qkv[rows, 2 * D + lanes : 2 * D + lanes + 128] = jnp.where(
        first, grad_v[0], grad_v[1]
    ).astype(BF16)


def mix_images(partners, mix, patches, mixed):
    for image in range(IMG):
        total = None
        for other in range(IMG):
            share = jnp.where(partners[image] == other, 1.0 - mix[image], 0.0)
            if image == other:
                share = share + mix[image]
            term = share * patches[other].astype(F32)
            total = term if total is None else total + term
        padding = jnp.zeros((ROWS - NPATCH, PATCH_DIM), F32)
        mixed[image * ROWS : (image + 1) * ROWS, :] = jnp.concatenate(
            [total, padding], axis=0
        ).astype(BF16)


def head_and_loss(
    image_count, stream, norms, partners, mix, labels, teacher, head, loss, feature, dlogits, dtop, dnorm
):
    picked = [
        stream[image * ROWS + NPATCH + kind : image * ROWS + NPATCH + kind + 1, :]
        for kind in range(2)
        for image in range(IMG)
    ]
    top = jnp.concatenate(picked + [jnp.zeros((2, D), F32)], axis=0)
    gain = norms[4 * L : 4 * L + 1, :]
    normed, _ = unit_norm(top)
    features = (normed * gain + norms[4 * L + 1 : 4 * L + 2, :]).astype(BF16)
    weights = head[...].astype(BF16)
    row = lax.broadcasted_iota(jnp.int32, (8, 2 * C), 0)
    lane = lax.broadcasted_iota(jnp.int32, (8, 2 * C), 1)
    is_class = row < IMG
    low_lane = jnp.where(is_class, 0, C)
    high_lane = jnp.where(is_class, C, jnp.where(row < 2 * IMG, 2 * C, 0))
    used = (lane >= low_lane) & (lane < high_lane)

    def log_softmax(values):
        values = jnp.where(used, values, LOWEST)
        shifted = values - jnp.max(values, axis=-1, keepdims=True)
        return shifted - jnp.log(jnp.sum(jnp.exp(shifted), axis=-1, keepdims=True))

    taught = jnp.concatenate([jnp.zeros((IMG, C), F32), teacher[...]], axis=1)
    taught = jnp.concatenate(
        [jnp.zeros((IMG, 2 * C), F32), taught, jnp.zeros((8 - 2 * IMG, 2 * C), F32)], axis=0
    )
    logits = nn(features, weights)
    student_log = log_softmax(jnp.where(is_class, logits, logits / TEMPER))
    teacher_log = log_softmax(taught / TEMPER)
    teacher_prob = jnp.exp(teacher_log)
    target = jnp.zeros((8, 2 * C), F32)
    for image in range(IMG):
        partner_label = labels[IMG - 1]
        for other in range(IMG - 1):
            partner_label = jnp.where(partners[image] == other, labels[other], partner_label)
        ours = jnp.where(lane == labels[image], mix[image], 0.0) + jnp.where(
            lane == partner_label, 1.0 - mix[image], 0.0
        )
        target = target + jnp.where(row == image, ours, 0.0)
    terms = jnp.where(
        is_class,
        -0.5 * target * student_log,
        0.5 * TEMPER * TEMPER * teacher_prob * (teacher_log - student_log),
    )
    terms = jnp.where(used, terms, 0.0)
    loss[...] = jnp.broadcast_to(jnp.sum(terms, axis=(0, 1), keepdims=True), (8, 128))
    wanted = jnp.where(is_class, target, teacher_prob)
    scale = jnp.where(is_class, 0.5 / image_count, 0.5 * TEMPER / image_count)
    grad_logits = (scale * jnp.where(used, jnp.exp(student_log) - wanted, 0.0)).astype(BF16)
    feature[...] = features.astype(F32)
    dlogits[...] = grad_logits.astype(F32)
    grad_top, grad_gain, grad_shift = norm_backward(nt(grad_logits, weights), top, gain)
    dtop[...] = grad_top
    dnorm[...] = jnp.concatenate([grad_gain, grad_shift, jnp.zeros((6, D), F32)], axis=0)


def forward_kernel(
    image_count,
    partners, mix, labels, patches, teacher, pos, head, norms, patch_w, attn_w, mlp_w,
    mixed_h, x_h, a_h, qkv_h, o_h, x1_h, a2_h, z_h, slope_h, loss, feature, dlogits, dtop, dnorm,
    mixed, x, a, qkv, o, x1, a2, z, slope, y, sems,
):
    mix_images(partners, mix, patches, mixed)
    embedded = nn(mixed[...], patch_w[...])
    for image in range(IMG):
        rows = slice(image * ROWS, (image + 1) * ROWS)
        x[rows, :] = embedded[rows] + pos[...]
    mixed_copy = pltpu.make_async_copy(mixed, mixed_h, sems.at[8])
    mixed_copy.start()

    def layer(depth, carry):
        norm = [norms[pl.ds(4 * depth + n, 1), :] for n in range(4)]
        a[...] = (unit_norm(x[...])[0] * norm[0] + norm[1]).astype(BF16)
        attn = attn_w.at[depth]
        for n in range(3):
            qkv[:, D * n : D * n + D] = nt(a[...], attn[2 * n : 2 * n + 2].reshape(D, D)).astype(BF16)
        for image in range(IMG):
            for pair in range(3):
                attend(qkv, o, image, pair)
        x1[...] = x[...] + nt(o[...], attn[6:8].reshape(D, D))
        a2[...] = (unit_norm(x1[...])[0] * norm[2] + norm[3]).astype(BF16)
        y[...] = x1[...]

        def block(m, carry):
            hidden = nn(a2[...], mlp_w[depth, 0, m].reshape(D, D))
            phi = 0.5 * (1.0 + lax.erf(hidden * 2.0**-0.5))
            low = (hidden * phi).astype(BF16)
            z[m] = low
            slope[m] = (phi + hidden * (jnp.exp(-0.5 * hidden * hidden) * 0.3989422804014327)).astype(BF16)
            y[...] += nt(low, mlp_w[depth, 1, m].reshape(D, D))
            return carry

        lax.fori_loop(0, BLOCKS, block, 0)
        saved = [(x, x_h), (a, a_h), (qkv, qkv_h), (o, o_h), (x1, x1_h), (a2, a2_h), (z, z_h), (slope, slope_h)]
        copies = [
            pltpu.make_async_copy(source, target.at[depth], sems.at[n])
            for n, (source, target) in enumerate(saved)
        ]
        for copy in copies:
            copy.start()
        for copy in copies:
            copy.wait()
        x[...] = y[...]
        return carry

    lax.fori_loop(0, L, layer, 0)
    mixed_copy.wait()
    head_and_loss(
        image_count, x, norms, partners, mix, labels, teacher, head, loss, feature, dlogits, dtop, dnorm
    )


SAVED = (
    ((ALL, PATCH_DIM), BF16),
    ((L, ALL, D), F32),
    ((L, ALL, D), BF16),
    ((L, ALL, 3 * D), BF16),
    ((L, ALL, D), BF16),
    ((L, ALL, D), F32),
    ((L, ALL, D), BF16),
    ((L, BLOCKS, ALL, D), BF16),
    ((L, BLOCKS, ALL, D), BF16),
)


def forward(image_count, *operands):
    small = (((8, 128), F32), ((8, D), F32), ((8, 2 * C), F32), ((8, D), F32), ((8, D), F32))
    scratch = [(SAVED[0])] + [(shape[1:], kind) for shape, kind in SAVED[1:]] + [((ALL, D), F32)]
    return pl.pallas_call(
        lambda *refs: forward_kernel(image_count, *refs),
        out_shape=[jax.ShapeDtypeStruct(*entry) for entry in SAVED + small],
        in_specs=[SMEM] * 3 + [VMEM] * 8,
        out_specs=[HBM] * len(SAVED) + [VMEM] * len(small),
        scratch_shapes=[pltpu.VMEM(*entry) for entry in scratch] + [pltpu.SemaphoreType.DMA((9,))],
        compiler_params=pltpu.CompilerParams(vmem_limit_bytes=60 * 2**20),
        name="forward",
    )(*operands)


def backward_kernel(
    dtop, norms, mixed, attn_w, mlp_w, x_h, a_h, qkv_h, o_h, x1_h, a2_h, z_h, slope_h,
    grad_patch, grad_attn, grad_mlp, grad_norm, grad_pos,
    dx, dy, low, dout, dqkv, x, a, qkv, o, x1, a2, z, slope, sems,
):
    saved = [(x_h, x), (a_h, a), (qkv_h, qkv), (o_h, o), (x1_h, x1), (a2_h, a2), (z_h, z), (slope_h, slope)]

    def fetch(depth, slot):
        return [
            pltpu.make_async_copy(source.at[depth], target.at[slot], sems.at[slot, n])
            for n, (source, target) in enumerate(saved)
        ]

    for copy in fetch(L - 1, 0):
        copy.start()
    dx[...] = jnp.zeros((ALL, D), F32)
    for kind in range(2):
        for image in range(IMG):
            row = image * ROWS + NPATCH + kind
            dx[row : row + 1, :] = dtop[kind * IMG + image : kind * IMG + image + 1, :]
    grad_norm[...] = jnp.zeros((16, D), F32)

    def layer(step, carry):
        depth = L - 1 - step
        slot = lax.rem(step, 2)
        for copy in fetch(depth, slot):
            copy.wait()

        @pl.when(step < L - 1)
        def _():
            for copy in fetch(depth - 1, 1 - slot):
                copy.start()

        low[...] = dx[...].astype(BF16)
        dy[...] = jnp.zeros((ALL, D), F32)

        def block(m, carry):
            grad_gelu = nn(low[...], mlp_w[depth, 1, m].reshape(D, D))
            grad_hidden = (grad_gelu * slope[slot, m].astype(F32)).astype(BF16)
            grad_mlp[depth, 0, m] = tn(a2[slot], grad_hidden).astype(BF16)
            grad_mlp[depth, 1, m] = tn(low[...], z[slot, m]).astype(BF16)
            dy[...] += nt(grad_hidden, mlp_w[depth, 0, m].reshape(D, D))
            return carry

        lax.fori_loop(0, BLOCKS, block, 0)
        grad_in, gain, shift = norm_backward(dy[...], x1[slot], norms[pl.ds(4 * depth + 2, 1), :])
        grad_norm[pl.ds(4 * depth + 2, 1), :] = gain
        grad_norm[pl.ds(4 * depth + 3, 1), :] = shift
        dx[...] += grad_in
        low[...] = dx[...].astype(BF16)
        attn = attn_w.at[depth]
        grad_attn[depth, 3 * D :] = tn(low[...], o[slot]).astype(BF16)
        dout[...] = nn(low[...], attn[6:8].reshape(D, D)).astype(BF16)
        for image in range(IMG):
            for pair in range(3):
                attend_backward(qkv.at[slot], dout, dqkv, image, pair)
        total = None
        for n in range(3):
            part = dqkv[:, D * n : D * n + D]
            grad_attn[depth, D * n : D * n + D] = tn(part, a[slot]).astype(BF16)
            term = nn(part, attn[2 * n : 2 * n + 2].reshape(D, D))
            total = term if total is None else total + term
        grad_in, gain, shift = norm_backward(total, x[slot], norms[pl.ds(4 * depth, 1), :])
        grad_norm[pl.ds(4 * depth, 1), :] = gain
        grad_norm[pl.ds(4 * depth + 1, 1), :] = shift
        dx[...] += grad_in
        return carry

    lax.fori_loop(0, L, layer, 0)
    grad_pos[...] = dx[0:ROWS] + dx[ROWS : 2 * ROWS] + dx[2 * ROWS :]
    grad_patch[...] = tn(mixed[...], dx[...].astype(BF16)).astype(BF16)


def backward(*operands):
    outs = (
        ((PATCH_DIM, D), BF16),
        ((L, 4 * D, D), BF16),
        ((L, 2, BLOCKS, D, D), BF16),
        ((16, D), F32),
        ((ROWS, D), F32),
    )
    scratch = [((ALL, D), F32), ((ALL, D), F32), ((ALL, D), BF16), ((ALL, D), BF16), ((ALL, 3 * D), BF16)]
    scratch += [((2,) + shape[1:], kind) for shape, kind in SAVED[1:]]
    return pl.pallas_call(
        backward_kernel,
        out_shape=[jax.ShapeDtypeStruct(*entry) for entry in outs],
        in_specs=[VMEM] * 5 + [HBM] * 8,
        out_specs=[VMEM] * len(outs),
        scratch_shapes=[pltpu.VMEM(*entry) for entry in scratch] + [pltpu.SemaphoreType.DMA((2, 8))],
        compiler_params=pltpu.CompilerParams(vmem_limit_bytes=62 * 2**20),
        name="backward",
    )(*operands)


def adam_update(weight, first_moment, second, grad_in, factor, step_rate):
    clipped = grad_in * factor
    first_moment = BETA_ONE * first_moment + (1.0 - BETA_ONE) * clipped
    second = BETA_TWO * second + (1.0 - BETA_TWO) * clipped * clipped
    adam_move = (
        first_moment
        / (1.0 - BETA_ONE**ADAM_STEP)
        / (jnp.sqrt(second / (1.0 - BETA_TWO**ADAM_STEP)) + ADAM_EPS)
    )
    return (weight - step_rate * (adam_move + DECAY * weight), first_moment, second)


def per_device(
    patches, partners, mix_weight, labels, teacher_logits,
    patch_weight, attn_weight, mlp_weight, positions, head_weight, norm_params,
    patch_first, attn_first, mlp_first, pos_first, head_first, norm_first,
    patch_second, attn_second, mlp_second, pos_second, head_second, norm_second,
):
    axes = ("dp", "mp")
    image_count = patches.shape[0] * lax.axis_size("dp") * lax.axis_size("mp")
    attn_t = jnp.swapaxes(attn_weight.astype(BF16), 1, 2)
    patch_low = lax.all_gather(patch_weight.astype(BF16), axes, axis=0, tiled=True)
    attn_low = lax.all_gather(attn_t, axes, axis=1, tiled=True)
    mlp_low = lax.all_gather(mlp_weight.astype(BF16), "dp", axis=2, tiled=True)
    mlp_low = lax.all_gather(mlp_low, "mp", axis=2, tiled=False)
    positions_last = jnp.concatenate(
        [positions[2:], positions[:2], jnp.zeros((ROWS - TOK, D), F32)], axis=0
    )
    attn_low = attn_low.reshape(L, 8, 4, 48, D)
    mlp_low = mlp_low.reshape(L, 2, BLOCKS, 8, 48, D)
    results = forward(
        image_count, partners, mix_weight, labels, patches, teacher_logits, positions_last,
        head_weight, norm_params, patch_low, attn_low, mlp_low,
    )
    saved, (loss, feature, dlogits, dtop, dnorm) = results[: len(SAVED)], results[len(SAVED) :]
    features = lax.all_gather(feature.astype(BF16), axes, axis=0, tiled=True)
    all_dlogits = lax.all_gather(dlogits.astype(BF16), axes, axis=0, tiled=True)
    head_sum = tn(features, all_dlogits)
    grad_patch, grad_attn, grad_mlp, grad_norm, grad_pos = backward(
        dtop, norm_params, saved[0], attn_low, mlp_low, *saved[1:]
    )
    patch_share = lax.psum_scatter(grad_patch.astype(F32), axes, scatter_dimension=0, tiled=True)
    attn_share = lax.psum_scatter(grad_attn.astype(F32), axes, scatter_dimension=1, tiled=True)
    mlp_share = lax.psum_scatter(grad_mlp.astype(F32), "mp", scatter_dimension=2, tiled=True)
    mlp_share = lax.psum_scatter(mlp_share, "dp", scatter_dimension=3, tiled=True)
    attn_share = jnp.swapaxes(attn_share, 1, 2)
    mlp_share = mlp_share.reshape(mlp_weight.shape)
    grad_norms = jnp.concatenate([grad_norm[: 4 * L], dnorm[:2]], axis=0)
    pos_sum, norm_sum, loss_sum = lax.psum(
        (jnp.concatenate([grad_pos[NPATCH:TOK], grad_pos[:NPATCH]], axis=0), grad_norms, loss[0, 0]), axes
    )
    own_squares = (
        jnp.sum(patch_share * patch_share)
        + jnp.sum(attn_share * attn_share)
        + jnp.sum(mlp_share * mlp_share)
    )
    shared = jnp.sum(pos_sum * pos_sum) + jnp.sum(head_sum * head_sum) + jnp.sum(norm_sum * norm_sum)
    global_norm = jnp.sqrt(lax.psum(own_squares, axes) + shared)
    factor = jnp.minimum(1.0, MAX_NORM / global_norm)
    weights = (patch_weight, attn_weight, mlp_weight, positions, head_weight, norm_params)
    firsts = (patch_first, attn_first, mlp_first, pos_first, head_first, norm_first)
    seconds = (patch_second, attn_second, mlp_second, pos_second, head_second, norm_second)
    grads = (patch_share, attn_share, mlp_share, pos_sum, head_sum, norm_sum)
    updated = [
        adam_update(weights[n], firsts[n], seconds[n], grads[n], factor, STEP_RATES[n]) for n in range(6)
    ]
    return (loss_sum, global_norm, *(entry[kind] for kind in range(3) for entry in updated))


def solution(mesh):
    images = (P(("dp", "mp"), None, None), P(("dp", "mp")), P(("dp", "mp")), P(("dp", "mp")), P(("dp", "mp"), None))
    weights = (P(("dp", "mp"), None), P(None, None, ("dp", "mp")), P(None, None, "dp", "mp"), P(), P(), P())
    return jax.shard_map(
        per_device,
        mesh=mesh,
        in_specs=images + weights * 3,
        out_specs=(P(), P()) + weights * 3,
        check_vma=False,
    )
```

time: 984 us -> 805 us (0.82)
  blocking collectives: 83.5 us -> 419 us
  waiting for transfers between devices: 528 us -> 221 us
  matrix products: 152 us -> 1.61 us
  local copies, waits for them, and re-layouts: 112 us -> 14.1 us
  Pallas kernels: 0 us -> 97.1 us
  other arithmetic: 75.7 us -> 29.1 us
    unnamed x9 -> x8, waiting for transfers between devices: 338 us -> 0.14 us
    unnamed x0 -> x1, blocking collectives: none -> 247 us
    dot_general x62 -> x1, matrix products: 152 us -> 1.61 us  [tn(): lax.dot_general(left, right, (((0,), (0,)), ((), ())), preferred_element_...]
    pallas_call x0 -> x2, Pallas kernels: none -> 97.1 us  [the longest x1 59.1 us: backward(): pl.pallas_call(backward_kernel, out_shape=[jax.ShapeDtypeStruct(*entry) f...]
    all_gather x1 -> x3, blocking collectives: 42.8 us -> 130 us  [the longest x1 45.2 us: per_device(): lax.all_gather(patch_weight.astype(BF16), axes, axis=0, tiled=True)]
    all_gather x3, waiting for transfers between devices: 85.1 us -> 114 us  [the longest x1 51.2 us: per_device(): mlp_low = lax.all_gather(mlp_low, 'mp', axis=2, tiled=False)]
    reshape x16 -> x0, local copies, waits for them, and re-layouts: 28.7 us -> none  [the longest x6 12 us: layer_backward(): grad_attended = matmul_nt(grad_branch, attn_layer[:, 3 * D:]).astype(jnp....]
    another operation x10 -> x0, other arithmetic: 27.3 us -> none  [the longest x4 20.5 us: per_device(): grad_mlp = jnp.stack(mlp_grads)]
  transfers between devices with their start and end apart: 7 -> 7, of which waited for: 7 -> 4; matrix products, arithmetic and copies ran while one was open for 12% -> 3% of each run, Pallas kernels for 0% -> 0%
where the time goes in v1:
time: 805 us; the launch traced here: 803 us
  blocking collectives  419 us (52%)
  waiting for transfers between devices  221 us (27%)
  Pallas kernels  97.1 us (12%)
  other arithmetic  29.1 us (4%)
  between operations  20.2 us (3%)
  local copies, waits for them, and re-layouts  14.1 us (2%)
    unnamed x1, blocking collectives  247 us
    reduce_scatter x1, waiting for transfers between devices, per_device(): lax.psum_scatter(grad_attn.astype(F32), axes, scatter_dimension=1, tiled=...  107 us
    pallas_call x1, Pallas kernels, backward(): pl.pallas_call(backward_kernel, out_shape=[jax.ShapeDtypeStruct(*entry) f...  59.1 us
    all_gather x1, waiting for transfers between devices, per_device(): mlp_low = lax.all_gather(mlp_low, 'mp', axis=2, tiled=False)  51.2 us
    all_gather x1, waiting for transfers between devices, per_device(): mlp_low = lax.all_gather(mlp_weight.astype(BF16), 'dp', axis=2, tiled=True)  47.8 us
    all_gather x1, blocking collectives, per_device(): lax.all_gather(patch_weight.astype(BF16), axes, axis=0, tiled=True)  45.2 us
    all_gather x1, blocking collectives, per_device(): features = lax.all_gather(feature.astype(BF16), axes, axis=0, tiled=True)  43.3 us
    all_gather x1, blocking collectives, per_device(): all_dlogits = lax.all_gather(dlogits.astype(BF16), axes, axis=0, tiled=True)  41.9 us
  transfers between devices with their start and end apart: 7, of which 4 were waited for; matrix products, arithmetic and copies ran while one was open for 3% of the time, Pallas kernels for 0%

profile of v1, /device:TPU:1, one launch (start us, length us, event | category | flops | bytes accessed | tf_op | source)
XLA Modules:
  0.0 802.8 jit_solution(10465732351422364892)
XLA Ops:
  7.2 0.0 all-gather.7.cloned.1.call-start
  7.3 1.9 convert_element_type.26
  9.1 0.0 all-gather.7.cloned.1.call-update
  9.2 0.0 all-gather.5.cloned.1.call-start
  9.2 1.6 convert_bitcast_fusion
  10.8 0.0 all-gather.9.cloned.1.call-start
  10.9 47.8 %all-gather.7.cloned.1.call-done = bf16[3,2,384,384]{3,2,1,0:T(8,128)(2,1)} async-done(((bf16[3,2,48,384]{3,2,1,0:T(8,128)(2,1)}), bf16[3,2,384,384]{3,2,1,0:T(8,128)(2,1)}) %all-gather.7.cloned.1.call-update) | async-done | bytes 1769488 | tf_op jit(solution)/shard_map/all_gather | solution.py:399
  58.7 0.0 all-reduce.6.cloned.1.call-start
  58.8 0.7 slice.21
  59.5 2.5 copy.44.refs_6_
  62.1 0.1 pad.6.clone
  62.2 0.8 maximum_maximum_fusion.refs_5_
  63.0 45.2 %all_gather.21.refs_8_ = bf16[768,384]{1,0:T(8,128)(2,1)} all-gather(bf16[24,384]{1,0:T(8,128)(2,1)S(1)} %convert_element_type.24), channel_id=1, replica_groups=mesh['dp'=8,'mp'=4] {'dp','mp'}, dimensions={0}, use_global_device_ids=true | all-gather | bytes 608256 | tf_op jit(solution)/shard_map/all_gather | solution.py:397
  108.2 14.8 %all-gather.5.cloned.1.call-done = bf16[3,1536,384]{2,1,0:T(8,128)(2,1)} async-done(((bf16[3,48,384]{2,1,0:T(8,128)(2,1)}), bf16[3,1536,384]{2,1,0:T(8,128)(2,1)}) %all-gather.5.cloned.1.call-update) | async-done | bytes 3538960 | tf_op jit(solution)/shard_map/all_gather | solution.py:398
  123.1 51.2 %all-gather.9.cloned.1.call-done = bf16[3,2,1536,384]{3,2,1,0:T(8,128)(2,1)} async-done(((bf16[3,2,384,384]{3,2,1,0:T(8,128)(2,1)}), bf16[3,2,1536,384]{3,2,1,0:T(8,128)(2,1)}) %all-gather.9.cloned.1.call-update) | async-done | bytes 7077904 | tf_op jit(solution)/shard_map/all_gather | solution.py:400
  174.3 38.0 %forward.1 = (bf16[624,768]{1,0:T(8,128)(2,1)}, f32[3,624,384]{2,1,0:T(8,128)}, bf16[3,624,384]{2,1,0:T(8,128)(2,1)}, bf16[3,624,1152]{2,1,0:T(8,128)(2,1)}, bf1...) custom-call(s32[3]{0:T(128)} %refs_0_.1, ...), custom_call_target="tpu_custom_call" | custom-call | tf_op jit(solution)/shard_map/forward/pallas_call | solution.py:271
  212.3 59.1 %backward.1 = (bf16[768,384]{1,0:T(8,128)(2,1)}, bf16[3,1536,384]{2,1,0:T(8,128)(2,1)}, bf16[3,2,4,384,384]{4,3,2,1,0:T(8,128)(2,1)}, f32[16,384]{1,0:T(8,128)}, f32[208,384]{1,0:T(8,128)}) custom-call(f32[8,384]{1,0:T(8,128)} %get-tuple-element.40.dtop, f32[14,384]{1,0:T(8,128)} %norms.1, bf16[624,768]{1,0:T(8,128)(2,1)} %get-tuple-element.41.mixed, ...), custom_call_target="tpu_custom_call" | custom-call | tf_op jit(solution)/shard_map/backward/pallas_call | solution.py:365
  271.5 1.0 slice.25
  272.5 0.7 slice.24
  273.2 0.7 pad_maximum_fusion
  273.9 0.0 reduce-scatter.13.cloned.1.call-start
  274.0 0.6 dynamic-slice.1
  274.6 2.2 convert_element_type.27
  276.8 0.0 reduce-scatter.11.cloned.1.call-start
  276.8 246.9 %all-reduce.7 = f32[3,2,4,384,384]{4,3,2,1,0:T(8,128)} all-reduce(bf16[3,2,4,384,384]{4,3,2,1,0:T(8,128)(2,1)} %get-tuple-element.52), channel_id=5, replica_groups=mesh['dp'=8,'mp'=4] {'mp'}, use_global_device_ids=true, to_apply=%region_5.0.clone | all-reduce | flops 3538944 | bytes 21233664
  523.7 4.6 constant_dynamic-slice_fusion
  528.4 0.3 reduce-scatter.9.cloned.1.call-start
  528.6 1.7 copy-done.1
  530.4 3.4 convert_element_type.28
  533.8 1.2 slice.23
  535.0 0.7 slice.27
  535.7 43.3 %all_gather.26 = bf16[256,384]{1,0:T(8,128)(2,1)S(1)} all-gather(bf16[8,384]{1,0:T(8,128)(2,1)S(1)} %convert_element_type.30), channel_id=1, replica_groups=mesh['dp'=8,'mp'=4] {'dp','mp'}, dimensions={0}, use_global_device_ids=true | all-gather | bytes 202752 | tf_op jit(solution)/shard_map/all_gather | solution.py:411
  579.0 41.9 %all_gather.27 = bf16[256,2000]{1,0:T(8,128)(2,1)S(1)} all-gather(bf16[8,2000]{1,0:T(8,128)(2,1)S(1)} %convert_element_type.31), channel_id=1, replica_groups=mesh['dp'=8,'mp'=4] {'dp','mp'}, dimensions={0}, use_global_device_ids=true | all-gather | bytes 1056000 | tf_op jit(solution)/shard_map/all_gather | solution.py:412
  621.0 1.6 multiply_reduce_fusion
  622.6 1.6 multiply_reduce_fusion.2
  625.6 0.0 reduce-scatter.13.cloned.1.call-done
  625.6 1.4 multiply_reduce_fusion.4
  627.0 1.8 multiply_reduce_fusion.1
  628.7 107.1 %reduce-scatter.9.cloned.1.call-done = f32[3,48,384]{2,1,0:T(8,128)} async-done(((f32[3,1536,384]{2,1,0:T(8,128)}), f32[3,48,384]{2,1,0:T(8,128)}) %reduce-scatter.9.cloned.1.call-update) | async-done | bytes 221200 | tf_op jit(solution)/shard_map/reduce_scatter | solution.py:418
  735.8 1.6 multiply_reduce_fusion.3
  739.4 41.7 %all-reduce.2 = (f32[]{:T(128)}, f32[]{:T(128)}, f32[14,384]{1,0:T(8,128)S(1)}) all-reduce(f32[]{:T(128)} %bitcast.3, f32[]{:T(128)S(6)} %add.122, f32[14,384]{1,0:T(8,128)S(1)} %pad_maximum_fusion.1), channel_id=1, replica_groups=mesh['dp'=8,'mp'=4] {'dp','mp'}, use_global_device_ids=true, to_apply=%region_0.0 | all-reduce | flops 5378 | bytes 43024 | tf_op jit(solution)/shard_map/psum | solution.py:424
  781.1 0.6 multiply_reduce_fusion.5
  783.1 0.6 multiply_subtract_fusion.5
  783.8 6.8 multiply_subtract_fusion
  790.7 0.7 multiply_subtract_fusion.4
  791.4 0.9 multiply_subtract_fusion.3
  792.4 1.3 multiply_subtract_fusion.1
  793.7 1.1 multiply_subtract_fusion.2
  (70 shorter events, 0.3 us)
Async XLA Ops:
  7.2 51.6 %copy-start.4 = (f32[198,384]{1,0:T(8,128)S(1)}, f32[198,384]{1,0:T(8,128)}, u32[]{:S(2)}) copy-start(f32[198,384]{1,0:T(8,128)} %param.31) | copy-start | bytes 912388
  7.2 52.3 %copy-start = (f32[384,2000]{0,1:T(8,128)S(1)}, f32[384,2000]{0,1:T(8,128)}, u32[]{:S(2)}) copy-start(f32[384,2000]{0,1:T(8,128)} %param.32) | copy-start | bytes 9216004
  7.2 51.5 %all-gather.7.cloned.1.call-start = ((), (), s32[]{:S(2)}) async-start(), calls=%async_computation.4 | async-start | bytes 1990656 | tf_op jit(solution)/shard_map/all_gather | solution.py:399
  9.2 113.9 %all-gather.5.cloned.1.call-start = ((), (), s32[]{:S(2)}) async-start(), calls=%async_computation.3 | async-start | bytes 3649536 | tf_op jit(solution)/shard_map/all_gather | solution.py:398
  10.8 163.5 %all-gather.9.cloned.1.call-start = ((), (), s32[]{:S(2)}) async-start(), calls=%async_computation.8 | async-start | bytes 8847360 | tf_op jit(solution)/shard_map/all_gather | solution.py:400
  58.7 563.9 %all-reduce.6.cloned.1.call-start = ((), (), s32[]{:S(2)}) async-start(), calls=%async_computation.7 | async-start | bytes 614400 | tf_op jit(solution)/shard_map/psum | solution.py:424
  59.5 2.5 copy-start.17
  59.5 2.6 slice-start
  59.5 2.6 copy-start.7
  212.3 61.7 %copy-start.27 = (u32[32]{0:T(128)S(1)}, u32[32]{0:T(128)}, u32[]{:S(2)}) copy-start(u32[32]{0:T(128)} %constant.42) | copy-start | bytes 388
  273.9 351.6 %reduce-scatter.13.cloned.1.call-start = ((), (), s32[]{:S(2)}) async-start(), calls=%async_computation.9 | async-start | bytes 1216512
  276.8 350.2 %reduce-scatter.11.cloned.1.call-start = ((), (), s32[]{:S(2)}) async-start(), calls=%async_computation.6 | async-start | bytes 3981312 | tf_op jit(solution)/shard_map/reduce_scatter | solution.py:420
  528.4 2.0 copy-start.1
  528.4 207.4 %reduce-scatter.9.cloned.1.call-start = ((), (), s32[]{:S(2)}) async-start(), calls=%async_computation.5 | async-start | bytes 7299072 | tf_op jit(solution)/shard_map/reduce_scatter | solution.py:418
  533.7 2.0 copy-start.26
  533.7 2.0 copy-start.20
  533.8 45.3 %copy-start.23 = (f32[16,384]{1,0:T(8,128)S(1)}, f32[16,384]{1,0:T(8,128)}, u32[]{:S(2)}) copy-start(f32[16,384]{1,0:T(8,128)} %get-tuple-element.56) | copy-start | bytes 73732
  621.0 162.1 %copy-start.16 = (f32[14,384]{1,0:T(8,128)S(1)}, f32[14,384]{1,0:T(8,128)}, u32[]{:S(2)}) copy-start(f32[14,384]{1,0:T(8,128)} %norms.1) | copy-start | bytes 64516
  621.0 162.1 %copy-start.24 = (f32[14,384]{1,0:T(8,128)S(1)}, f32[14,384]{1,0:T(8,128)}, u32[]{:S(2)}) copy-start(f32[14,384]{1,0:T(8,128)} %param.39) | copy-start | bytes 64516
  621.0 162.1 %copy-start.25 = (f32[14,384]{1,0:T(8,128)S(1)}, f32[14,384]{1,0:T(8,128)}, u32[]{:S(2)}) copy-start(f32[14,384]{1,0:T(8,128)} %param.45) | copy-start | bytes 64516
  783.7 7.0 copy-start.18
  783.7 7.0 copy-start.19
  783.7 7.0 copy-start.21
  783.7 7.0 copy-start.22
  783.7 7.7 copy-start.8
  783.7 7.7 copy-start.9
  783.7 7.7 copy-start.14
  783.8 7.7 copy-start.15
  783.8 8.6 %copy-start.2 = (f32[3,2,48,384]{3,2,1,0:T(8,128)S(1)}, f32[3,2,48,384]{3,2,1,0:T(8,128)}, u32[]{:S(2)}) copy-start(f32[3,2,48,384]{3,2,1,0:T(8,128)} %param.30) | copy-start | bytes 1327108
  783.8 8.6 %copy-start.3 = (f32[3,2,1,48,384]{4,3,2,1,0:T(8,128)S(1)}, f32[3,2,1,48,384]{4,3,2,1,0:T(8,128)}, u32[]{:S(2)}) copy-start(f32[3,2,1,48,384]{4,3,2,1,0:T(8,128)} %reduce-scatter.11.cloned.1.call-done) | copy-start | bytes 1327108
  783.8 8.6 %copy-start.10 = (f32[3,2,48,384]{3,2,1,0:T(8,128)S(1)}, f32[3,2,48,384]{3,2,1,0:T(8,128)}, u32[]{:S(2)}) copy-start(f32[3,2,48,384]{3,2,1,0:T(8,128)} %param.36) | copy-start | bytes 1327108
  783.8 8.6 %copy-start.11 = (f32[3,2,48,384]{3,2,1,0:T(8,128)S(1)}, f32[3,2,48,384]{3,2,1,0:T(8,128)}, u32[]{:S(2)}) copy-start(f32[3,2,48,384]{3,2,1,0:T(8,128)} %param.42) | copy-start | bytes 1327108
  790.7 3.0 copy-start.5
  790.7 3.0 copy-start.6
  790.7 3.0 copy-start.12
  790.7 3.0 copy-start.13
Sparse Core Ops, SparseCore 0:
  10.9 47.7 all-gather.6
  62.2 60.7 all-gather.4
  124.6 49.6 all-gather.8
  274.1 125.2 all-reduce.5
  405.7 97.2 reduce-scatter.12
  528.5 83.0 reduce-scatter.10
  618.2 117.5 reduce-scatter.8

commit v2 on v1

--- a/solution.py
+++ b/solution.py
@@ -16,6 +16,13 @@
 ALL = IMG * ROWS
 BLOCKS = 4
 
+Z = 4
+Y = 2
+X = 2
+CORES = 2
+EVERY = slice(0, 2)
+PIECES = 11
+
 LN_EPS = 1e-06
 TEMPER = 3.0
 MAX_NORM = 0.02
@@ -32,6 +39,7 @@
 VMEM = pl.BlockSpec(memory_space=pltpu.VMEM)
 SMEM = pl.BlockSpec(memory_space=pltpu.SMEM)
 HBM = pl.BlockSpec(memory_space=pl.ANY)
+MESH = pl.DeviceIdType.MESH
 
 
 def nn(left, right):
@@ -63,6 +71,113 @@
         - normed * jnp.mean(scaled * normed, axis=-1, keepdims=True)
     )
     return grad_in, grad_gain, grad_shift
+
+
+class Place:
+    def __init__(self):
+        dp, mp = lax.axis_index("dp"), lax.axis_index("mp")
+        self.z, self.y = dp // Y, dp % Y
+        self.x, self.core = mp // CORES, mp % CORES
+
+    def at(self, dz=0, dy=0, dx=0, dcore=0):
+        z = lax.rem(self.z + dz, Z)
+        y = 1 - self.y if dy else self.y
+        x = 1 - self.x if dx else self.x
+        core = 1 - self.core if dcore else self.core
+        return {"dp": z * Y + y, "mp": x * CORES + core}
+
+    def partners(self):
+        column = [self.at(dz=step) for step in range(1, Z)]
+        return column + [self.at(dx=1), self.at(dy=1), self.at(dcore=1), self.at(dy=1, dx=1)]
+
+
+def greet(partners):
+    barrier = pltpu.get_barrier_semaphore()
+    for partner in partners:
+        pl.semaphore_signal(barrier, inc=1, device_id=partner, device_id_type=MESH)
+    pl.semaphore_wait(barrier, len(partners))
+
+
+class Gather:
+    def __init__(self, place, pieces, planes, send_sems, recv_sems):
+        self.place, self.pieces, self.planes = place, pieces, planes
+        self.send_sems, self.recv_sems = send_sems, recv_sems
+        self.started = []
+        self.done = set()
+
+    def copy(self, piece, n, region, target):
+        view = self.pieces[piece](*region)
+        return pltpu.make_async_remote_copy(
+            src_ref=view,
+            dst_ref=view,
+            send_sem=self.send_sems.at[piece, n],
+            recv_sem=self.recv_sems.at[piece, n],
+            device_id=target,
+            device_id_type=MESH,
+        )
+
+    def send(self, piece, n, region, **offset):
+        copy = self.copy(piece, n, region, self.place.at(**offset))
+        copy.start()
+        self.started.append(copy)
+
+    def recv(self, piece, n, region):
+        self.copy(piece, n, region, self.place.at(dcore=1)).wait_recv()
+
+    def step(self, piece, stage):
+        if (piece, stage) in self.done:
+            return
+        self.done.add((piece, stage))
+        z, y, x, core = self.place.z, self.place.y, self.place.x, self.place.core
+        far_y, far_x, sibling = 1 - y, 1 - x, 1 - core
+        column, low, high = slice(0, Z), slice(0, Z // 2), slice(Z // 2, Z)
+        if piece in self.planes:
+            if stage == 1:
+                self.send(piece, 3, (z, y, x, core), dx=1)
+                self.send(piece, 4, (z, y, x, core), dy=1)
+                self.send(piece, 6, (z, y, x, core), dy=1, dx=1)
+            if stage == 2:
+                self.recv(piece, 3, (z, y, far_x, core))
+                self.recv(piece, 4, (z, far_y, x, core))
+                self.recv(piece, 6, (z, far_y, far_x, core))
+                for hop in range(1, Z):
+                    self.send(piece, hop - 1, (z, EVERY, EVERY, core), dz=hop)
+            if stage == 4:
+                for hop in range(1, Z):
+                    self.recv(piece, hop - 1, (lax.rem(z + Z - hop, Z), EVERY, EVERY, core))
+                self.send(piece, 5, (column, EVERY, EVERY, core), dcore=1)
+            if stage == 5:
+                self.recv(piece, 5, (column, EVERY, EVERY, sibling))
+            return
+        if stage == 1:
+            for hop in range(1, Z):
+                self.send(piece, hop - 1, (z, y, x, core), dz=hop)
+        if stage == 2:
+            for hop in range(1, Z):
+                self.recv(piece, hop - 1, (lax.rem(z + Z - hop, Z), y, x, core))
+            self.send(piece, 3, (column, y, x, core), dx=1)
+            self.send(piece, 4, (column, y, x, core), dy=1)
+            self.send(piece, 5, (column, y, x, core), dcore=1)
+        if stage == 3:
+            self.recv(piece, 3, (column, y, far_x, core))
+            self.send(piece, 6, (low, y, far_x, core), dy=1)
+            self.send(piece, 8, (column, y, far_x, core), dcore=1)
+            self.recv(piece, 4, (column, far_y, x, core))
+            self.send(piece, 7, (high, far_y, x, core), dx=1)
+            self.send(piece, 9, (column, far_y, x, core), dcore=1)
+        if stage == 4:
+            self.recv(piece, 6, (low, far_y, far_x, core))
+            self.recv(piece, 7, (high, far_y, far_x, core))
+            self.send(piece, 10, (column, far_y, far_x, core), dcore=1)
+        if stage == 5:
+            self.recv(piece, 5, (column, y, x, sibling))
+            self.recv(piece, 8, (column, y, far_x, sibling))
+            self.recv(piece, 9, (column, far_y, x, sibling))
+            self.recv(piece, 10, (column, far_y, far_x, sibling))
+
+    def finish(self):
+        for copy in self.started:
+            copy.wait_send()
 
 
 def head_lanes(shape, head):
@@ -166,7 +281,7 @@
     taught = jnp.concatenate(
         [jnp.zeros((IMG, 2 * C), F32), taught, jnp.zeros((8 - 2 * IMG, 2 * C), F32)], axis=0
     )
-    logits = nn(features, weights)
+    logits = nt(features, weights)
     student_log = log_softmax(jnp.where(is_class, logits, logits / TEMPER))
     teacher_log = log_softmax(taught / TEMPER)
     teacher_prob = jnp.exp(teacher_log)
@@ -191,65 +306,176 @@
     grad_logits = (scale * jnp.where(used, jnp.exp(student_log) - wanted, 0.0)).astype(BF16)
     feature[...] = features.astype(F32)
     dlogits[...] = grad_logits.astype(F32)
-    grad_top, grad_gain, grad_shift = norm_backward(nt(grad_logits, weights), top, gain)
+    grad_top, grad_gain, grad_shift = norm_backward(nn(grad_logits, weights), top, gain)
     dtop[...] = grad_top
     dnorm[...] = jnp.concatenate([grad_gain, grad_shift, jnp.zeros((6, D), F32)], axis=0)
 
 
-def forward_kernel(
-    image_count,
-    partners, mix, labels, patches, teacher, pos, head, norms, patch_w, attn_w, mlp_w,
-    mixed_h, x_h, a_h, qkv_h, o_h, x1_h, a2_h, z_h, slope_h, loss, feature, dlogits, dtop, dnorm,
-    mixed, x, a, qkv, o, x1, a2, z, slope, y, sems,
-):
+ATTN_SHAPE = (L, Z, Y, X, CORES, 48, D)
+MLP_SHAPE = (L, 2, X, CORES, Z, Y, 48, D)
+PATCH_SHAPE = (Z, Y, X, CORES, 32, D)
+N_PIECES = 1 + 3 * L
+PLANES = (1 + 3 * (L - 1),)
+QUEUE = tuple(n for n in range(N_PIECES) if n not in PLANES)
+
+
+def gather_views(patch_w, attn_w, mlp_w):
+    def attn(depth):
+        return lambda z, y, x, core: attn_w.at[depth, z, y, x, core]
+
+    def mlp(depth, part):
+        return lambda z, y, x, core: mlp_w.at[depth, part, x, core, z, y]
+
+    views = [lambda z, y, x, core: patch_w.at[z, y, x, core]]
+    for depth in range(L):
+        views += [attn(depth), mlp(depth, 0), mlp(depth, 1)]
+    return views
+
+
+def forward_kernel(image_count, sharded, *refs):
+    (
+        partners, mix, labels, patches_h, teacher, pos, head_h, norms, patch_in, attn_in, mlp_in,
+        mixed_h, x_h, a_h, qkv_h, o_h, x1_h, a2_h, z_h, slope_h, attn_h, mlp_h,
+        loss, feature, dlogits, dtop, dnorm,
+        mixed, x, a, qkv, o, x1, a2, z, slope, attn_w, mlp_w,
+        patches, head, stream, patch_w, in_sems, out_sems, *rest,
+    ) = refs
+    outgoing = []
+
+    def keep(source, target):
+        copy = pltpu.make_async_copy(source, target, out_sems.at[len(outgoing)])
+        copy.start()
+        outgoing.append(copy)
+
+    if sharded:
+        patch_all, patch_s, attn_s, mlp_s, send_sems, recv_sems = rest
+        loads = [(attn_in, attn_s), (mlp_in, mlp_s), (patch_in, patch_s)]
+    else:
+        loads = [(attn_in, attn_w), (mlp_in, mlp_w), (patch_in, patch_w)]
+    loads += [(patches_h, patches), (head_h, head)]
+    loads = [
+        pltpu.make_async_copy(source, target, in_sems.at[n]) for n, (source, target) in enumerate(loads)
+    ]
+    for copy in loads:
+        copy.start()
+
+    if sharded:
+        place = Place()
+        gather = Gather(place, gather_views(patch_all, attn_w, mlp_w), PLANES, send_sems, recv_sems)
+        mine = (place.z, place.y, place.x, place.core)
+        loads[2].wait()
+        patch_all[mine] = jnp.concatenate([patch_s[...], jnp.zeros((8, D), F32)], axis=0).astype(BF16)
+        loads[0].wait()
+        for depth in range(L):
+            attn_w[(depth,) + mine] = attn_s[depth].astype(BF16)
+        loads[1].wait()
+        for depth in range(L):
+            for part in range(2):
+                mlp_w[depth, part, place.x, place.core, place.z, place.y] = mlp_s[depth, part].astype(BF16)
+        greet(place.partners())
+        for piece in PLANES + QUEUE:
+            gather.step(piece, 1)
+
+    def ahead(n, stage):
+        if sharded and n < len(QUEUE):
+            gather.step(QUEUE[n], stage)
+
+    def need(piece):
+        if not sharded:
+            return
+        if piece in PLANES:
+            for stage in (4, 5):
+                gather.step(piece, stage)
+            return
+        n = QUEUE.index(piece)
+        ahead(n + 1, 2)
+        ahead(n, 3)
+        ahead(n + 2, 2)
+        ahead(n + 1, 3)
+        ahead(n, 4)
+        ahead(n, 5)
+
+    def between(piece):
+        if not sharded:
+            return
+        later = [n for n in range(len(QUEUE)) if QUEUE[n] > piece]
+        if later:
+            ahead(later[0] + 2, 2)
+            ahead(later[0] + 1, 3)
+
+    if sharded:
+        ahead(0, 2)
+        for piece in PLANES:
+            gather.step(piece, 2)
+        ahead(1, 2)
+        ahead(0, 3)
+    else:
+        for n in range(3):
+            loads[n].wait()
+    loads[3].wait()
     mix_images(partners, mix, patches, mixed)
+    keep(mixed, mixed_h)
+    need(0)
+    if sharded:
+        for n in range(Z * Y * X):
+            block = patch_all[n // 4, n // 2 % 2, n % 2].astype(F32)
+            patch_w[48 * n : 48 * n + 48, :] = jnp.concatenate([block[0, :24], block[1, :24]], axis=0).astype(BF16)
     embedded = nn(mixed[...], patch_w[...])
+    added = jnp.concatenate([pos[2:TOK, :], pos[0:2, :], jnp.zeros((ROWS - TOK, D), F32)], axis=0)
     for image in range(IMG):
         rows = slice(image * ROWS, (image + 1) * ROWS)
-        x[rows, :] = embedded[rows] + pos[...]
-    mixed_copy = pltpu.make_async_copy(mixed, mixed_h, sems.at[8])
-    mixed_copy.start()
-
-    def layer(depth, carry):
-        norm = [norms[pl.ds(4 * depth + n, 1), :] for n in range(4)]
-        a[...] = (unit_norm(x[...])[0] * norm[0] + norm[1]).astype(BF16)
-        attn = attn_w.at[depth]
+        x[0, rows, :] = embedded[rows] + added
+    for depth in range(L):
+        norm = [norms[4 * depth + n : 4 * depth + n + 1, :] for n in range(4)]
+        first = 1 + 3 * depth
+        keep(x.at[depth], x_h.at[depth])
+        a[depth] = (unit_norm(x[depth])[0] * norm[0] + norm[1]).astype(BF16)
+        keep(a.at[depth], a_h.at[depth])
+        need(first)
         for n in range(3):
-            qkv[:, D * n : D * n + D] = nt(a[...], attn[2 * n : 2 * n + 2].reshape(D, D)).astype(BF16)
+            qkv[depth, :, D * n : D * n + D] = nt(a[depth], attn_w[depth, n].reshape(D, D)).astype(BF16)
+        keep(qkv.at[depth], qkv_h.at[depth])
+        keep(attn_w.at[depth], attn_h.at[depth])
         for image in range(IMG):
             for pair in range(3):
-                attend(qkv, o, image, pair)
-        x1[...] = x[...] + nt(o[...], attn[6:8].reshape(D, D))
-        a2[...] = (unit_norm(x1[...])[0] * norm[2] + norm[3]).astype(BF16)
-        y[...] = x1[...]
-
-        def block(m, carry):
-            hidden = nn(a2[...], mlp_w[depth, 0, m].reshape(D, D))
+                attend(qkv.at[depth], o.at[depth], image, pair)
+            if image == 1:
+                between(first)
+        keep(o.at[depth], o_h.at[depth])
+        x1[depth] = x[depth] + nt(o[depth], attn_w[depth, 3].reshape(D, D))
+        keep(x1.at[depth], x1_h.at[depth])
+        a2[depth] = (unit_norm(x1[depth])[0] * norm[2] + norm[3]).astype(BF16)
+        keep(a2.at[depth], a2_h.at[depth])
+        need(first + 1)
+
+        def widen(m, carry):
+            hidden = nn(a2[depth], mlp_w[depth, 0, m // 2, lax.rem(m, 2)].reshape(D, D))
             phi = 0.5 * (1.0 + lax.erf(hidden * 2.0**-0.5))
-            low = (hidden * phi).astype(BF16)
-            z[m] = low
-            slope[m] = (phi + hidden * (jnp.exp(-0.5 * hidden * hidden) * 0.3989422804014327)).astype(BF16)
-            y[...] += nt(low, mlp_w[depth, 1, m].reshape(D, D))
+            z[depth, m] = (hidden * phi).astype(BF16)
+            density = jnp.exp(-0.5 * hidden * hidden) * 0.3989422804014327
+            slope[depth, m] = (phi + hidden * density).astype(BF16)
             return carry
 
-        lax.fori_loop(0, BLOCKS, block, 0)
-        saved = [(x, x_h), (a, a_h), (qkv, qkv_h), (o, o_h), (x1, x1_h), (a2, a2_h), (z, z_h), (slope, slope_h)]
-        copies = [
-            pltpu.make_async_copy(source, target.at[depth], sems.at[n])
-            for n, (source, target) in enumerate(saved)
-        ]
-        for copy in copies:
-            copy.start()
-        for copy in copies:
-            copy.wait()
-        x[...] = y[...]
-        return carry
-
-    lax.fori_loop(0, L, layer, 0)
-    mixed_copy.wait()
+        lax.fori_loop(0, BLOCKS, widen, 0)
+        keep(z.at[depth], z_h.at[depth])
+        keep(slope.at[depth], slope_h.at[depth])
+        need(first + 2)
+        keep(mlp_w.at[depth], mlp_h.at[depth])
+        total = x1[depth]
+        for m in range(BLOCKS):
+            total = total + nt(z[depth, m], mlp_w[depth, 1, m // 2, m % 2].reshape(D, D))
+        if depth + 1 < L:
+            x[depth + 1] = total
+        else:
+            stream[...] = total
+    loads[4].wait()
     head_and_loss(
-        image_count, x, norms, partners, mix, labels, teacher, head, loss, feature, dlogits, dtop, dnorm
-    )
+        image_count, stream, norms, partners, mix, labels, teacher, head, loss, feature, dlogits, dtop, dnorm
+    )
+    for copy in outgoing:
+        copy.wait()
+    if sharded:
+        gather.finish()
 
 
 SAVED = (
@@ -262,19 +488,38 @@
     ((L, ALL, D), BF16),
     ((L, BLOCKS, ALL, D), BF16),
     ((L, BLOCKS, ALL, D), BF16),
+    (ATTN_SHAPE, BF16),
+    (MLP_SHAPE, BF16),
 )
-
-
-def forward(image_count, *operands):
-    small = (((8, 128), F32), ((8, D), F32), ((8, 2 * C), F32), ((8, D), F32), ((8, D), F32))
-    scratch = [(SAVED[0])] + [(shape[1:], kind) for shape, kind in SAVED[1:]] + [((ALL, D), F32)]
+SMALL = (((8, 128), F32), ((8, D), F32), ((8, 2 * C), F32), ((8, D), F32), ((8, D), F32))
+
+
+def forward(image_count, sharded, *operands):
+    scratch = SAVED + (
+        ((IMG, NPATCH, PATCH_DIM), BF16),
+        ((2 * C, D), F32),
+        ((ALL, D), F32),
+        ((PATCH_DIM, D), BF16),
+    )
+    scratch = [pltpu.VMEM(*entry) for entry in scratch]
+    scratch += [pltpu.SemaphoreType.DMA((5,)), pltpu.SemaphoreType.DMA((1 + 10 * L,))]
+    if sharded:
+        scratch += [
+            pltpu.VMEM(PATCH_SHAPE, BF16),
+            pltpu.VMEM((PATCH_DIM // (Z * Y * X * CORES), D), F32),
+            pltpu.VMEM((L, 48, D), F32),
+            pltpu.VMEM((L, 2, 48, D), F32),
+            pltpu.SemaphoreType.DMA((N_PIECES, PIECES)),
+            pltpu.SemaphoreType.DMA((N_PIECES, PIECES)),
+        ]
+    params = dict(collective_id=0, has_side_effects=True) if sharded else {}
     return pl.pallas_call(
-        lambda *refs: forward_kernel(image_count, *refs),
-        out_shape=[jax.ShapeDtypeStruct(*entry) for entry in SAVED + small],
-        in_specs=[SMEM] * 3 + [VMEM] * 8,
-        out_specs=[HBM] * len(SAVED) + [VMEM] * len(small),
-        scratch_shapes=[pltpu.VMEM(*entry) for entry in scratch] + [pltpu.SemaphoreType.DMA((9,))],
-        compiler_params=pltpu.CompilerParams(vmem_limit_bytes=60 * 2**20),
+        lambda *refs: forward_kernel(image_count, sharded, *refs),
+        out_shape=[jax.ShapeDtypeStruct(*entry) for entry in SAVED + SMALL],
+        in_specs=[SMEM] * 3 + [HBM, VMEM, VMEM, HBM, VMEM] + [HBM] * 3,
+        out_specs=[HBM] * len(SAVED) + [VMEM] * len(SMALL),
+        scratch_shapes=scratch,
+        compiler_params=pltpu.CompilerParams(vmem_limit_bytes=62 * 2**20, **params),
         name="forward",
     )(*operands)
 
@@ -316,11 +561,11 @@
         dy[...] = jnp.zeros((ALL, D), F32)
 
         def block(m, carry):
-            grad_gelu = nn(low[...], mlp_w[depth, 1, m].reshape(D, D))
+            grad_gelu = nn(low[...], mlp_w[depth, 1, m // 2, lax.rem(m, 2)].reshape(D, D))
             grad_hidden = (grad_gelu * slope[slot, m].astype(F32)).astype(BF16)
             grad_mlp[depth, 0, m] = tn(a2[slot], grad_hidden).astype(BF16)
             grad_mlp[depth, 1, m] = tn(low[...], z[slot, m]).astype(BF16)
-            dy[...] += nt(grad_hidden, mlp_w[depth, 0, m].reshape(D, D))
+            dy[...] += nt(grad_hidden, mlp_w[depth, 0, m // 2, lax.rem(m, 2)].reshape(D, D))
             return carry
 
         lax.fori_loop(0, BLOCKS, block, 0)
@@ -331,7 +576,7 @@
         low[...] = dx[...].astype(BF16)
         attn = attn_w.at[depth]
         grad_attn[depth, 3 * D :] = tn(low[...], o[slot]).astype(BF16)
-        dout[...] = nn(low[...], attn[6:8].reshape(D, D)).astype(BF16)
+        dout[...] = nn(low[...], attn[3].reshape(D, D)).astype(BF16)
         for image in range(IMG):
             for pair in range(3):
                 attend_backward(qkv.at[slot], dout, dqkv, image, pair)
@@ -339,7 +584,7 @@
         for n in range(3):
             part = dqkv[:, D * n : D * n + D]
             grad_attn[depth, D * n : D * n + D] = tn(part, a[slot]).astype(BF16)
-            term = nn(part, attn[2 * n : 2 * n + 2].reshape(D, D))
+            term = nn(part, attn[n].reshape(D, D))
             total = term if total is None else total + term
         grad_in, gain, shift = norm_backward(total, x[slot], norms[pl.ds(4 * depth, 1), :])
         grad_norm[pl.ds(4 * depth, 1), :] = gain
@@ -361,7 +606,7 @@
         ((ROWS, D), F32),
     )
     scratch = [((ALL, D), F32), ((ALL, D), F32), ((ALL, D), BF16), ((ALL, D), BF16), ((ALL, 3 * D), BF16)]
-    scratch += [((2,) + shape[1:], kind) for shape, kind in SAVED[1:]]
+    scratch += [((2,) + shape[1:], kind) for shape, kind in SAVED[1:9]]
     return pl.pallas_call(
         backward_kernel,
         out_shape=[jax.ShapeDtypeStruct(*entry) for entry in outs],
@@ -393,26 +638,26 @@
 ):
     axes = ("dp", "mp")
     image_count = patches.shape[0] * lax.axis_size("dp") * lax.axis_size("mp")
-    attn_t = jnp.swapaxes(attn_weight.astype(BF16), 1, 2)
-    patch_low = lax.all_gather(patch_weight.astype(BF16), axes, axis=0, tiled=True)
-    attn_low = lax.all_gather(attn_t, axes, axis=1, tiled=True)
-    mlp_low = lax.all_gather(mlp_weight.astype(BF16), "dp", axis=2, tiled=True)
-    mlp_low = lax.all_gather(mlp_low, "mp", axis=2, tiled=False)
-    positions_last = jnp.concatenate(
-        [positions[2:], positions[:2], jnp.zeros((ROWS - TOK, D), F32)], axis=0
-    )
-    attn_low = attn_low.reshape(L, 8, 4, 48, D)
-    mlp_low = mlp_low.reshape(L, 2, BLOCKS, 8, 48, D)
+    sharded = (lax.axis_size("dp"), lax.axis_size("mp")) == (Z * Y, X * CORES)
+    attn_t = jnp.swapaxes(attn_weight, 1, 2)
+    if sharded:
+        weights_in = (patch_weight, attn_t, mlp_weight)
+    else:
+        patch_low = lax.all_gather(patch_weight.astype(BF16), axes, axis=0, tiled=True)
+        attn_low = lax.all_gather(attn_t.astype(BF16), axes, axis=1, tiled=True)
+        mlp_low = lax.all_gather(mlp_weight.astype(BF16), "dp", axis=2, tiled=True)
+        mlp_low = lax.all_gather(mlp_low, "mp", axis=2, tiled=False)
+        weights_in = (patch_low, attn_low.reshape(ATTN_SHAPE), mlp_low.reshape(MLP_SHAPE))
     results = forward(
-        image_count, partners, mix_weight, labels, patches, teacher_logits, positions_last,
-        head_weight, norm_params, patch_low, attn_low, mlp_low,
+        image_count, sharded, partners, mix_weight, labels, patches, teacher_logits, positions,
+        head_weight.T, norm_params, *weights_in,
     )
     saved, (loss, feature, dlogits, dtop, dnorm) = results[: len(SAVED)], results[len(SAVED) :]
     features = lax.all_gather(feature.astype(BF16), axes, axis=0, tiled=True)
     all_dlogits = lax.all_gather(dlogits.astype(BF16), axes, axis=0, tiled=True)
-    head_sum = tn(features, all_dlogits)
+    head_sum = tn(all_dlogits, features).T
     grad_patch, grad_attn, grad_mlp, grad_norm, grad_pos = backward(
-        dtop, norm_params, saved[0], attn_low, mlp_low, *saved[1:]
+        dtop, norm_params, saved[0], *saved[9:], *saved[1:9]
     )
     patch_share = lax.psum_scatter(grad_patch.astype(F32), axes, scatter_dimension=0, tiled=True)
     attn_share = lax.psum_scatter(grad_attn.astype(F32), axes, scatter_dimension=1, tiled=True)

time: 805 us -> 674 us (0.84)
  waiting for transfers between devices: 221 us -> 110 us
  blocking collectives: 419 us -> 374 us
  Pallas kernels: 97.1 us -> 131 us
    all_gather x3 -> x0, waiting for transfers between devices: 114 us -> none  [the longest x1 51.2 us: per_device(): mlp_low = lax.all_gather(mlp_low, 'mp', axis=2, tiled=False)]
    all_gather x1 -> x0, blocking collectives: 45.2 us -> none  [per_device(): lax.all_gather(patch_weight.astype(BF16), axes, axis=0, tiled=True)]
    pallas_call x1, Pallas kernels: 38 us -> 71.4 us  [forward(): pl.pallas_call(lambda *refs: forward_kernel(image_count, sharded, *refs),...]
  transfers between devices with their start and end apart: 7 -> 4, of which waited for: 4 -> 1; matrix products, arithmetic and copies ran while one was open for 3% -> 3% of each run, Pallas kernels for 0% -> 0%
where the time goes in v2:
time: 674 us; the launch traced here: 672 us
  blocking collectives  374 us (55%)
  Pallas kernels  131 us (19%)
  waiting for transfers between devices  110 us (16%)
  other arithmetic  24.7 us (4%)
  between operations  19.8 us (3%)
  local copies, waits for them, and re-layouts  10.6 us (2%)
    unnamed x1, blocking collectives  248 us
    reduce_scatter x1, waiting for transfers between devices, per_device(): lax.psum_scatter(grad_attn.astype(F32), axes, scatter_dimension=1, tiled=...  110 us
    pallas_call x1, Pallas kernels, forward(): pl.pallas_call(lambda *refs: forward_kernel(image_count, sharded, *refs),...  71.4 us
    pallas_call x1, Pallas kernels, backward(): pl.pallas_call(backward_kernel, out_shape=[jax.ShapeDtypeStruct(*entry) f...  59.2 us
    all_gather x1, blocking collectives, per_device(): features = lax.all_gather(feature.astype(BF16), axes, axis=0, tiled=True)  42.5 us
    psum x1, blocking collectives, per_device(): lax.psum((jnp.concatenate([grad_pos[NPATCH:TOK], grad_pos[:NPATCH]], axis...  41.7 us
    all_gather x1, blocking collectives, per_device(): all_dlogits = lax.all_gather(dlogits.astype(BF16), axes, axis=0, tiled=True)  41.6 us
  transfers between devices with their start and end apart: 4, of which 1 were waited for; matrix products, arithmetic and copies ran while one was open for 3% of the time, Pallas kernels for 0%

profile of v2, /device:TPU:1, one launch (start us, length us, event | category | flops | bytes accessed | tf_op | source)
XLA Modules:
  0.0 672.2 jit_solution(7448811728495863463)
XLA Ops:
  7.2 0.0 all-reduce.6.cloned.1.call-start
  7.2 71.4 %forward.1 = (bf16[624,768]{1,0:T(8,128)(2,1)}, f32[3,624,384]{2,1,0:T(8,128)}, bf16[3,624,384]{2,1,0:T(8,128)(2,1)}, bf16[3,624,1152]{2,1,0:T(8,128)(2,1)}, bf1...) custom-call(s32[3]{0:T(128)} %refs_0_.1, ...), custom_call_target="tpu_custom_call" | custom-call | tf_op jit(solution)/shard_map/forward/pallas_call | solution.py:516
  78.6 59.2 %backward.1 = (bf16[768,384]{1,0:T(8,128)(2,1)}, bf16[3,1536,384]{2,1,0:T(8,128)(2,1)}, bf16[3,2,4,384,384]{4,3,2,1,0:T(8,128)(2,1)}, f32[16,384]{1,0:T(8,128)}, f32[208,384]{1,0:T(8,128)}) custom-call(f32[8,384]{1,0:T(8,128)} %get-tuple-element.42.dtop, f32[14,384]{1,0:T(8,128)} %norms.1, bf16[624,768]{1,0:T(8,128)(2,1)} %get-tuple-element.43.mixed, ...), custom_call_target="tpu_custom_call" | custom-call | tf_op jit(solution)/shard_map/backward/pallas_call | solution.py:610
  137.8 1.0 slice.17
  138.8 0.7 slice.16
  139.6 0.7 pad_maximum_fusion
  140.3 0.0 all-reduce.6.cloned.1.call-update
  140.3 0.0 reduce-scatter.13.cloned.1.call-start
  140.4 2.2 convert_element_type.15
  142.5 0.0 reduce-scatter.13.cloned.1.call-update
  142.6 0.0 reduce-scatter.11.cloned.1.call-start
  142.6 0.0 copy-start.23
  142.6 248.5 %all-reduce.7 = f32[3,2,4,384,384]{4,3,2,1,0:T(8,128)} all-reduce(bf16[3,2,4,384,384]{4,3,2,1,0:T(8,128)(2,1)} %get-tuple-element.56), channel_id=4, replica_groups=mesh['dp'=8,'mp'=4] {'mp'}, use_global_device_ids=true, to_apply=%region_5.0.clone | all-reduce | flops 3538944 | bytes 21233664
  391.1 0.6 dynamic-slice.1
  391.7 4.6 constant_dynamic-slice_fusion
  396.3 0.0 reduce-scatter.11.cloned.1.call-update
  396.3 0.3 reduce-scatter.9.cloned.1.call-start
  396.7 1.7 copy-done
  398.3 3.4 convert_element_type.16
  401.7 0.0 reduce-scatter.9.cloned.1.call-update
  401.7 1.2 slice.15
  403.0 0.7 slice.19
  403.7 42.5 %all_gather.6 = bf16[256,384]{1,0:T(8,128)(2,1)S(1)} all-gather(bf16[8,384]{1,0:T(8,128)(2,1)S(1)} %convert_element_type.18), channel_id=1, replica_groups=mesh['dp'=8,'mp'=4] {'dp','mp'}, dimensions={0}, use_global_device_ids=true | all-gather | bytes 202752 | tf_op jit(solution)/shard_map/all_gather | solution.py:656
  446.2 41.6 %all_gather.7 = bf16[256,2000]{1,0:T(8,128)(2,1)S(1)} all-gather(bf16[8,2000]{1,0:T(8,128)(2,1)S(1)} %convert_element_type.19), channel_id=1, replica_groups=mesh['dp'=8,'mp'=4] {'dp','mp'}, dimensions={0}, use_global_device_ids=true | all-gather | bytes 1056000 | tf_op jit(solution)/shard_map/all_gather | solution.py:657
  487.8 1.6 multiply_reduce_fusion
  489.4 1.6 multiply_reduce_fusion.2
  492.4 0.0 reduce-scatter.13.cloned.1.call-done
  492.4 1.4 multiply_reduce_fusion.4
  493.8 1.7 multiply_reduce_fusion.1
  495.5 110.1 %reduce-scatter.9.cloned.1.call-done = f32[3,48,384]{2,1,0:T(8,128)} async-done(((f32[3,1536,384]{2,1,0:T(8,128)}), f32[3,48,384]{2,1,0:T(8,128)}) %reduce-scatter.9.cloned.1.call-update) | async-done | bytes 221200 | tf_op jit(solution)/shard_map/reduce_scatter | solution.py:663
  605.6 1.6 multiply_reduce_fusion.3
  609.1 41.7 %all-reduce.2 = (f32[]{:T(128)}, f32[]{:T(128)}, f32[14,384]{1,0:T(8,128)S(1)}) all-reduce(f32[]{:T(128)} %bitcast.2, f32[]{:T(128)S(6)} %add.122, f32[14,384]{1,0:T(8,128)S(1)} %pad_maximum_fusion.1), channel_id=1, replica_groups=mesh['dp'=8,'mp'=4] {'dp','mp'}, use_global_device_ids=true, to_apply=%region_0.0 | all-reduce | flops 5378 | bytes 43024 | tf_op jit(solution)/shard_map/psum | solution.py:669
  650.8 0.6 multiply_reduce_fusion.5
  652.8 0.6 multiply_subtract_fusion.5
  653.5 0.0 copy-start.6
  653.5 0.0 copy-start.12
  653.5 0.0 copy-start.13
  653.5 0.0 copy-start.1
  653.5 0.0 copy-start.7
  653.6 0.0 copy-start.8
  653.6 6.8 %multiply_subtract_fusion = (f32[384,2000]{0,1:T(8,128)}, f32[384,2000]{0,1:T(8,128)}, f32[384,2000]{0,1:T(8,128)}) fusion(f32[384,2000]{0,1:T(8,128)} %param.32, f32[384,2000]{0,1:T(8,128)S(1)} %get-tuple-element.84, f32[]{:T(128)S(6)} %min_shard_map.3, f32[384,2000]{0,1:T(8,128)} %param.38, f32[384,2000]{0,1:T(8,128)} %param.44), kind=kLoop, calls=%fused_computation.2 | loop fusion | flops 12288000 | bytes 21504004 | tf_op jit(solution)/shard_map/sub | solution.py:630
  660.5 0.0 copy-start.3
  660.5 0.0 copy-start.9
  660.5 0.0 copy-start.10
  660.5 0.7 multiply_subtract_fusion.4
  661.2 0.9 multiply_subtract_fusion.3
  662.1 1.3 multiply_subtract_fusion.1
  663.5 1.1 multiply_subtract_fusion.2
  (42 shorter events, 0.1 us)
Async XLA Ops:
  7.2 482.2 %all-reduce.6.cloned.1.call-start = ((), (), s32[]{:S(2)}) async-start(), calls=%async_computation.5 | async-start | bytes 614400 | tf_op jit(solution)/shard_map/psum | solution.py:669
  140.3 352.1 %reduce-scatter.13.cloned.1.call-start = ((), (), s32[]{:S(2)}) async-start(), calls=%async_computation.6 | async-start | bytes 1216512
  142.6 351.2 %reduce-scatter.11.cloned.1.call-start = ((), (), s32[]{:S(2)}) async-start(), calls=%async_computation.4 | async-start | bytes 3981312 | tf_op jit(solution)/shard_map/reduce_scatter | solution.py:665
  142.6 248.5 %copy-start.23 = (u32[32]{0:T(128)S(1)}, u32[32]{0:T(128)}, u32[]{:S(2)}) copy-start(u32[32]{0:T(128)} %constant.42) | copy-start | bytes 388
  396.3 2.0 copy-start
  396.3 209.2 %reduce-scatter.9.cloned.1.call-start = ((), (), s32[]{:S(2)}) async-start(), calls=%async_computation.3 | async-start | bytes 7299072 | tf_op jit(solution)/shard_map/reduce_scatter | solution.py:663
  401.7 2.0 copy-start.22
  401.7 2.0 copy-start.16
  401.7 44.4 %copy-start.19 = (f32[16,384]{1,0:T(8,128)S(1)}, f32[16,384]{1,0:T(8,128)}, u32[]{:S(2)}) copy-start(f32[16,384]{1,0:T(8,128)} %get-tuple-element.60) | copy-start | bytes 73732
  487.8 165.0 %copy-start.11 = (f32[14,384]{1,0:T(8,128)S(1)}, f32[14,384]{1,0:T(8,128)}, u32[]{:S(2)}) copy-start(f32[14,384]{1,0:T(8,128)} %norms.1) | copy-start | bytes 64516
  487.8 165.0 %copy-start.20 = (f32[14,384]{1,0:T(8,128)S(1)}, f32[14,384]{1,0:T(8,128)}, u32[]{:S(2)}) copy-start(f32[14,384]{1,0:T(8,128)} %param.39) | copy-start | bytes 64516
  487.8 165.0 %copy-start.21 = (f32[14,384]{1,0:T(8,128)S(1)}, f32[14,384]{1,0:T(8,128)}, u32[]{:S(2)}) copy-start(f32[14,384]{1,0:T(8,128)} %param.45) | copy-start | bytes 64516
  653.5 7.0 %copy-start.14 = (f32[24,384]{1,0:T(8,128)S(1)}, f32[24,384]{1,0:T(8,128)}, u32[]{:S(2)}) copy-start(f32[24,384]{1,0:T(8,128)} %refs_8_.1) | copy-start | bytes 110596
  653.5 7.0 %copy-start.15 = (f32[24,384]{1,0:T(8,128)S(1)}, f32[24,384]{1,0:T(8,128)}, u32[]{:S(2)}) copy-start(f32[24,384]{1,0:T(8,128)} %reduce-scatter.13.cloned.1.call-done) | copy-start | bytes 110596
  653.5 7.0 %copy-start.17 = (f32[24,384]{1,0:T(8,128)S(1)}, f32[24,384]{1,0:T(8,128)}, u32[]{:S(2)}) copy-start(f32[24,384]{1,0:T(8,128)} %param.34) | copy-start | bytes 110596
  653.5 7.0 %copy-start.18 = (f32[24,384]{1,0:T(8,128)S(1)}, f32[24,384]{1,0:T(8,128)}, u32[]{:S(2)}) copy-start(f32[24,384]{1,0:T(8,128)} %param.40) | copy-start | bytes 110596
  653.5 7.7 %copy-start.5 = (f32[3,48,384]{2,1,0:T(8,128)S(1)}, f32[3,48,384]{2,1,0:T(8,128)}, u32[]{:S(2)}) copy-start(f32[3,48,384]{2,1,0:T(8,128)} %reduce-scatter.9.cloned.1.call-done) | copy-start | bytes 663556
  653.5 7.7 %copy-start.6 = (f32[3,384,48]{1,2,0:T(8,128)S(1)}, f32[3,384,48]{1,2,0:T(8,128)}, u32[]{:S(2)}) copy-start(f32[3,384,48]{1,2,0:T(8,128)} %param.29) | copy-start | bytes 663556
  653.5 7.7 %copy-start.12 = (f32[3,384,48]{1,2,0:T(8,128)S(1)}, f32[3,384,48]{1,2,0:T(8,128)}, u32[]{:S(2)}) copy-start(f32[3,384,48]{1,2,0:T(8,128)} %param.35) | copy-start | bytes 663556
  653.5 7.7 %copy-start.13 = (f32[3,384,48]{1,2,0:T(8,128)S(1)}, f32[3,384,48]{1,2,0:T(8,128)}, u32[]{:S(2)}) copy-start(f32[3,384,48]{1,2,0:T(8,128)} %param.41) | copy-start | bytes 663556
  653.5 8.6 %copy-start.1 = (f32[3,2,48,384]{3,2,1,0:T(8,128)S(1)}, f32[3,2,48,384]{3,2,1,0:T(8,128)}, u32[]{:S(2)}) copy-start(f32[3,2,48,384]{3,2,1,0:T(8,128)} %refs_10_.1) | copy-start | bytes 1327108
  653.5 8.6 %copy-start.2 = (f32[3,2,1,48,384]{4,3,2,1,0:T(8,128)S(1)}, f32[3,2,1,48,384]{4,3,2,1,0:T(8,128)}, u32[]{:S(2)}) copy-start(f32[3,2,1,48,384]{4,3,2,1,0:T(8,128)} %reduce-scatter.11.cloned.1.call-done) | copy-start | bytes 1327108
  653.5 8.6 %copy-start.7 = (f32[3,2,48,384]{3,2,1,0:T(8,128)S(1)}, f32[3,2,48,384]{3,2,1,0:T(8,128)}, u32[]{:S(2)}) copy-start(f32[3,2,48,384]{3,2,1,0:T(8,128)} %param.36) | copy-start | bytes 1327108
  653.6 8.6 %copy-start.8 = (f32[3,2,48,384]{3,2,1,0:T(8,128)S(1)}, f32[3,2,48,384]{3,2,1,0:T(8,128)}, u32[]{:S(2)}) copy-start(f32[3,2,48,384]{3,2,1,0:T(8,128)} %param.42) | copy-start | bytes 1327108
  660.5 3.0 copy-start.3
  660.5 3.0 copy-start.4
  660.5 3.0 copy-start.9
  660.5 3.0 copy-start.10
Sparse Core Ops, SparseCore 0:
  140.4 128.8 all-reduce.5
  275.8 97.3 reduce-scatter.12
  396.5 84.0 reduce-scatter.10
  487.0 118.5 reduce-scatter.8

commit v3 on v2

--- a/solution.py
+++ b/solution.py
@@ -180,6 +180,86 @@
             copy.wait_send()
 
 
+def add_into(target, *terms):
+    def body(n, carry):
+        total = target[n].astype(F32)
+        for term in terms:
+            total = total + term[n].astype(F32)
+        target[n] = total.astype(target.dtype)
+        return carry
+
+    lax.fori_loop(0, target.shape[0], body, 0)
+
+
+class Scatter:
+    def __init__(self, place, pieces, send_sems, recv_sems):
+        self.place, self.pieces = place, pieces
+        self.send_sems, self.recv_sems = send_sems, recv_sems
+        self.started = []
+
+    def copy(self, piece, n, source, target, **offset):
+        return pltpu.make_async_remote_copy(
+            src_ref=source,
+            dst_ref=target,
+            send_sem=self.send_sems.at[piece, n],
+            recv_sem=self.recv_sems.at[piece, n],
+            device_id=self.place.at(**offset),
+            device_id_type=MESH,
+        )
+
+    def send(self, piece, n, source, target, **offset):
+        copy = self.copy(piece, n, source, target, **offset)
+        copy.start()
+        self.started.append(copy)
+
+    def recv(self, piece, n, target):
+        self.copy(piece, n, target, target, dcore=1).wait_recv()
+        return target
+
+    def step(self, piece, stage):
+        z, y, x, core = self.place.z, self.place.y, self.place.x, self.place.core
+        far_y, far_x, sibling = 1 - y, 1 - x, 1 - core
+        column, low, high = slice(0, Z), slice(0, Z // 2), slice(Z // 2, Z)
+        part = self.pieces[piece]
+        grad = part["grad"]
+        if stage == 1:
+            self.send(piece, 0, grad(column, EVERY, EVERY, sibling), part["half"], dcore=1)
+        if stage == 2:
+            add_into(grad(column, EVERY, EVERY, core), self.recv(piece, 0, part["half"]))
+            self.send(piece, 1, grad(low, far_y, far_x, core), part["corner"](0), dy=1)
+            self.send(piece, 2, grad(high, far_y, far_x, core), part["corner"](1), dx=1)
+        if stage == 3:
+            add_into(grad(low, y, far_x, core), self.recv(piece, 1, part["corner"](0)))
+            self.send(piece, 3, grad(column, y, far_x, core), part["side"](0), dx=1)
+            add_into(grad(high, far_y, x, core), self.recv(piece, 2, part["corner"](1)))
+            self.send(piece, 4, grad(column, far_y, x, core), part["side"](1), dy=1)
+        if stage == 4:
+            sides = [self.recv(piece, 3 + n, part["side"](n)) for n in range(2)]
+            add_into(grad(column, y, x, core), *sides)
+            for hop in range(1, Z):
+                self.send(
+                    piece, 4 + hop, grad(lax.rem(z + hop, Z), y, x, core), part["hop"](hop - 1), dz=hop
+                )
+        if stage == 5:
+            total = grad(z, y, x, core)[...].astype(F32)
+            for hop in range(1, Z):
+                total = total + self.recv(piece, 4 + hop, part["hop"](hop - 1))[...].astype(F32)
+            part["share"](total)
+
+    def finish(self):
+        for copy in self.started:
+            copy.wait_send()
+
+
+def round_rows(source, target):
+    def body(n, carry):
+        rows = pl.ds(n * ROWS, ROWS)
+        target[rows, :] = source[rows, :].astype(target.dtype)
+        return carry
+
+    lax.fori_loop(0, IMG, body, 0)
+
+
 def head_lanes(shape, head):
     lane = lax.broadcasted_iota(jnp.int32, shape, len(shape) - 1)
     return lane < 64 if head == 0 else lane >= 64
@@ -524,96 +604,307 @@
     )(*operands)
 
 
-def backward_kernel(
-    dtop, norms, mixed, attn_w, mlp_w, x_h, a_h, qkv_h, o_h, x1_h, a2_h, z_h, slope_h,
-    grad_patch, grad_attn, grad_mlp, grad_norm, grad_pos,
-    dx, dy, low, dout, dqkv, x, a, qkv, o, x1, a2, z, slope, sems,
-):
-    saved = [(x_h, x), (a_h, a), (qkv_h, qkv), (o_h, o), (x1_h, x1), (a2_h, a2), (z_h, z), (slope_h, slope)]
-
-    def fetch(depth, slot):
-        return [
-            pltpu.make_async_copy(source.at[depth], target.at[slot], sems.at[slot, n])
-            for n, (source, target) in enumerate(saved)
-        ]
-
-    for copy in fetch(L - 1, 0):
-        copy.start()
+SMALL_SHAPE = (Z, Y, X, CORES, 8, D)
+N_GRADS = 2 * L + 2
+PATCH_PIECE = 2 * L
+SMALL_PIECE = 2 * L + 1
+MLP_DUE = (3, 5, 7, 10, 14)
+ATTN_DUE = (8, 10, 12, 14, 17)
+LAST_DUE = (20, 21, 22, 23, 24)
+HEAD_DUE = (0, 1, 2, 3, 4)
+
+
+def scatter_pieces(grads, halves, corners, sides, hops, shares):
+    patch, attn, mlp, small = range(4)
+
+    def flat(kind):
+        return dict(
+            grad=lambda z, y, x, core: grads[kind].at[z, y, x, core],
+            half=halves[kind],
+            corner=lambda n: corners[kind].at[n],
+            side=lambda n: sides[kind].at[n],
+            hop=lambda n: hops[kind].at[n],
+            share=shares[kind],
+        )
+
+    def layered(kind, depth, grad):
+        return dict(
+            grad=grad,
+            half=halves[kind].at[depth],
+            corner=lambda n: corners[kind].at[depth, n],
+            side=lambda n: sides[kind].at[depth, n],
+            hop=lambda n: hops[kind].at[depth, n],
+            share=lambda total: shares[kind](depth, total),
+        )
+
+    pieces = []
+    for depth in reversed(range(L)):
+        pieces.append(
+            layered(mlp, depth, lambda z, y, x, core, depth=depth: grads[mlp].at[depth, :, x, core, z, y])
+        )
+        pieces.append(layered(attn, depth, lambda z, y, x, core, depth=depth: grads[attn].at[depth, z, y, x, core]))
+    return pieces + [flat(patch), flat(small)]
+
+
+def scatter_scratch():
+    cases = (((), (), 32, BF16), ((L,), (), 48, BF16), ((L,), (2,), 48, BF16), ((), (), 8, F32))
+    halves = [
+        pltpu.VMEM((Z, Y, X, 32, D), BF16),
+        pltpu.VMEM((L, Z, Y, X, 48, D), BF16),
+        pltpu.VMEM((L, 2, X, Z, Y, 48, D), BF16),
+        pltpu.VMEM((Z, Y, X, 8, D), F32),
+    ]
+    corners = [pltpu.VMEM(lead + (2,) + parts + (Z // 2, rows, D), kind) for lead, parts, rows, kind in cases]
+    sides = [pltpu.VMEM(lead + (2,) + parts + (Z, rows, D), kind) for lead, parts, rows, kind in cases]
+    hops = [pltpu.VMEM(lead + (Z - 1,) + parts + (rows, D), kind) for lead, parts, rows, kind in cases]
+    return halves + corners + sides + hops
+
+
+def backward_kernel(sharded, *refs):
+    dtop, norms, mixed_h, *refs = refs
+    held, refs = refs[:10], refs[10:]
+    if sharded:
+        loss, feature, dlogits, dnorm, *refs = refs
+        patch_share, attn_share, mlp_share, head_sum, pos_sum, norm_sum, stats, *refs = refs
+    else:
+        grad_patch, grad_attn, grad_mlp, grad_norm, grad_pos, *refs = refs
+    dx, dy, low, dout, dqkv, mixed, *refs = refs
+    kept, sems, refs = refs[:10], refs[10], refs[11:]
+    x, a, qkv, o, x1, a2, z, slope, attn_w, mlp_w = kept
+    names = ("x", "a", "qkv", "o", "x1", "a2", "z", "slope", "attn", "mlp")
+
+    def fetch(depth, *wanted):
+        if depth < 0:
+            return
+        for name in wanted:
+            n = names.index(name)
+            pltpu.make_async_copy(held[n].at[depth], kept[n], sems.at[n]).start()
+
+    def arrive(depth, *wanted):
+        for name in wanted:
+            n = names.index(name)
+            pltpu.make_async_copy(held[n].at[depth], kept[n], sems.at[n]).wait()
+
+    fetch(L - 1, "mlp", "slope", "a2", "z", "x1", "o", "attn", "qkv", "a", "x")
+    mixed_copy = pltpu.make_async_copy(mixed_h, mixed, sems.at[len(names)])
+    mixed_copy.start()
+    due = {}
+    if sharded:
+        grad_patch, grad_attn, grad_mlp, grad_small, grad_norm, all_features, all_dlogits, packed, gathered, squares, *refs = refs
+        buffers, refs = refs[:16], refs[16:]
+        send_sems, recv_sems, head_send, head_recv, last_send, last_recv = refs
+        place = Place()
+        mine = (place.z, place.y, place.x, place.core)
+
+        def count(total):
+            flat = total.reshape(-1, D)
+            squares[0:1, :] += jnp.sum(flat * flat, axis=0, keepdims=True)
+
+        def share_patch(total):
+            patch_share[...] = total[: patch_share.shape[0]]
+            count(total)
+
+        def share_attn(depth, total):
+            attn_share[depth] = total
+            count(total)
+
+        def share_mlp(depth, total):
+            mlp_share[depth] = total
+            count(total)
+
+        def share_small(total):
+            gathered[mine + (slice(None), slice(0, D))] = total
+
+        scatter = Scatter(
+            place,
+            scatter_pieces(
+                (grad_patch, grad_attn, grad_mlp, grad_small),
+                *(buffers[4 * n : 4 * n + 4] for n in range(4)),
+                (share_patch, share_attn, share_mlp, share_small),
+            ),
+            send_sems,
+            recv_sems,
+        )
+        heads = Gather(
+            place,
+            [
+                lambda z, y, x, core: all_features.at[z, y, x, core],
+                lambda z, y, x, core: all_dlogits.at[z, y, x, core],
+            ],
+            (), head_send, head_recv,
+        )
+        for turn in range(L):
+            for stage in range(5):
+                due.setdefault(10 * turn + MLP_DUE[stage], []).append((scatter, 2 * turn, stage + 1))
+                due.setdefault(10 * turn + ATTN_DUE[stage], []).append((scatter, 2 * turn + 1, stage + 1))
+        for stage in range(5):
+            for piece in (PATCH_PIECE, SMALL_PIECE):
+                due.setdefault(10 * (L - 1) + LAST_DUE[stage] - 10, []).append((scatter, piece, stage + 1))
+            for piece in (1, 0):
+                due.setdefault(HEAD_DUE[stage] - 1, []).append((heads, piece, stage + 1))
+        squares[...] = jnp.zeros_like(squares)
+        all_features[mine] = feature[...]
+        all_dlogits[mine] = dlogits[...]
+        greet(place.partners())
+
+    def point(now):
+        for who, piece, stage in due.pop(now, ()):
+            who.step(piece, stage)
+
+    point(-1)
     dx[...] = jnp.zeros((ALL, D), F32)
     for kind in range(2):
         for image in range(IMG):
             row = image * ROWS + NPATCH + kind
             dx[row : row + 1, :] = dtop[kind * IMG + image : kind * IMG + image + 1, :]
     grad_norm[...] = jnp.zeros((16, D), F32)
-
-    def layer(step, carry):
-        depth = L - 1 - step
-        slot = lax.rem(step, 2)
-        for copy in fetch(depth, slot):
-            copy.wait()
-
-        @pl.when(step < L - 1)
-        def _():
-            for copy in fetch(depth - 1, 1 - slot):
-                copy.start()
-
-        low[...] = dx[...].astype(BF16)
-        dy[...] = jnp.zeros((ALL, D), F32)
-
-        def block(m, carry):
-            grad_gelu = nn(low[...], mlp_w[depth, 1, m // 2, lax.rem(m, 2)].reshape(D, D))
-            grad_hidden = (grad_gelu * slope[slot, m].astype(F32)).astype(BF16)
-            grad_mlp[depth, 0, m] = tn(a2[slot], grad_hidden).astype(BF16)
-            grad_mlp[depth, 1, m] = tn(low[...], z[slot, m]).astype(BF16)
-            dy[...] += nt(grad_hidden, mlp_w[depth, 0, m // 2, lax.rem(m, 2)].reshape(D, D))
-            return carry
-
-        lax.fori_loop(0, BLOCKS, block, 0)
-        grad_in, gain, shift = norm_backward(dy[...], x1[slot], norms[pl.ds(4 * depth + 2, 1), :])
-        grad_norm[pl.ds(4 * depth + 2, 1), :] = gain
-        grad_norm[pl.ds(4 * depth + 3, 1), :] = shift
+    for turn in range(L):
+        depth = L - 1 - turn
+        start = 10 * turn
+        round_rows(dx, low)
+        arrive(depth, "mlp", "slope", "a2", "z")
+        total = None
+        for m in range(BLOCKS):
+            at = (m // 2, m % 2)
+            grad_gelu = nn(low[...], mlp_w[(1,) + at].reshape(D, D))
+            grad_hidden = (grad_gelu * slope[m].astype(F32)).astype(BF16)
+            grad_mlp[(depth, 0) + at] = tn(a2[...], grad_hidden).astype(BF16).reshape(Z, Y, 48, D)
+            grad_mlp[(depth, 1) + at] = tn(low[...], z[m]).astype(BF16).reshape(Z, Y, 48, D)
+            term = nt(grad_hidden, mlp_w[(0,) + at].reshape(D, D))
+            dy[...] = term if m == 0 else dy[...] + term
+            point(start + m)
+        fetch(depth - 1, "mlp", "slope", "a2", "z")
+        arrive(depth, "x1", "o", "attn")
+        grad_in, gain, shift = norm_backward(dy[...], x1[...], norms[4 * depth + 2 : 4 * depth + 3, :])
+        grad_norm[4 * depth + 2 : 4 * depth + 3, :] = gain
+        grad_norm[4 * depth + 3 : 4 * depth + 4, :] = shift
         dx[...] += grad_in
-        low[...] = dx[...].astype(BF16)
-        attn = attn_w.at[depth]
-        grad_attn[depth, 3 * D :] = tn(low[...], o[slot]).astype(BF16)
-        dout[...] = nn(low[...], attn[3].reshape(D, D)).astype(BF16)
+        round_rows(dx, low)
+        point(start + 4)
+        grad_attn[depth, 3] = tn(low[...], o[...]).astype(BF16).reshape(Y, X, CORES, 48, D)
+        dout[...] = nn(low[...], attn_w[3].reshape(D, D)).astype(BF16)
+        fetch(depth - 1, "x1", "o")
+        arrive(depth, "qkv")
         for image in range(IMG):
             for pair in range(3):
-                attend_backward(qkv.at[slot], dout, dqkv, image, pair)
+                attend_backward(qkv, dout, dqkv, image, pair)
+            point(start + 5 + image)
+        fetch(depth - 1, "qkv")
+        arrive(depth, "a", "x")
+        for n in range(3):
+            part = dqkv[:, D * n : D * n + D]
+            grad_attn[depth, n] = tn(part, a[...]).astype(BF16).reshape(Y, X, CORES, 48, D)
+        point(start + 8)
         total = None
         for n in range(3):
-            part = dqkv[:, D * n : D * n + D]
-            grad_attn[depth, D * n : D * n + D] = tn(part, a[slot]).astype(BF16)
-            term = nn(part, attn[n].reshape(D, D))
+            term = nn(dqkv[:, D * n : D * n + D], attn_w[n].reshape(D, D))
             total = term if total is None else total + term
-        grad_in, gain, shift = norm_backward(total, x[slot], norms[pl.ds(4 * depth, 1), :])
-        grad_norm[pl.ds(4 * depth, 1), :] = gain
-        grad_norm[pl.ds(4 * depth + 1, 1), :] = shift
+        fetch(depth - 1, "attn", "a")
+        grad_in, gain, shift = norm_backward(total, x[...], norms[4 * depth : 4 * depth + 1, :])
+        grad_norm[4 * depth : 4 * depth + 1, :] = gain
+        grad_norm[4 * depth + 1 : 4 * depth + 2, :] = shift
         dx[...] += grad_in
+        fetch(depth - 1, "x")
+        point(start + 9)
+    total = dx[0:ROWS] + dx[ROWS : 2 * ROWS] + dx[2 * ROWS :]
+    round_rows(dx, low)
+    mixed_copy.wait()
+    patch = tn(mixed[...], low[...])
+    rows = PATCH_DIM // (Z * Y * X * CORES)
+    for n in range(Z * Y * X * CORES):
+        block = jnp.concatenate([patch[rows * n : rows * n + rows], jnp.zeros((32 - rows, D), F32)], axis=0)
+        grad_patch[n // 8, n // 4 % 2, n // 2 % 2, n % 2] = block.astype(BF16)
+    if not sharded:
+        grad_pos[...] = total
+        return
+    small = [total[8 * n : 8 * n + 8] for n in range(ROWS // 8)]
+    small += [grad_norm[0:8, :], jnp.concatenate([grad_norm[8:12, :], dnorm[0:2, :], jnp.zeros((2, D), F32)], axis=0)]
+    small.append(jnp.concatenate([loss[...], jnp.zeros((8, D - 128), F32)], axis=1))
+    for n in range(Z * Y * X * CORES):
+        grad_small[n // 8, n // 4 % 2, n // 2 % 2, n % 2] = small[n] if n < len(small) else jnp.zeros((8, D), F32)
+    left = sorted(due)
+    for now in left[:2]:
+        point(now)
+    features = all_features[...].reshape(-1, D).astype(BF16)
+    per_plane = packed.shape[0] // Z
+
+    def pack(n, carry):
+        packed[pl.ds(n * per_plane, per_plane), :] = all_dlogits[n].reshape(per_plane, -1).astype(BF16)
         return carry
 
-    lax.fori_loop(0, L, layer, 0)
-    grad_pos[...] = dx[0:ROWS] + dx[ROWS : 2 * ROWS] + dx[2 * ROWS :]
-    grad_patch[...] = tn(mixed[...], dx[...].astype(BF16)).astype(BF16)
-
-
-def backward(*operands):
-    outs = (
-        ((PATCH_DIM, D), BF16),
-        ((L, 4 * D, D), BF16),
-        ((L, 2, BLOCKS, D, D), BF16),
-        ((16, D), F32),
-        ((ROWS, D), F32),
+    lax.fori_loop(0, Z, pack, 0)
+    for n in range(0, 2 * C, 512):
+        lanes = slice(n, min(n + 512, 2 * C))
+        part = tn(packed[:, lanes], features)
+        head_sum[lanes, :] = part
+        squares[1:2, :] += jnp.sum(part * part, axis=0, keepdims=True)
+    for now in left[2:]:
+        point(now)
+    own = jnp.sum(squares[0:1, :], axis=(0, 1), keepdims=True)
+    gathered[mine + (slice(None), slice(D, D + 128))] = jnp.broadcast_to(own, (8, 128))
+    last = Gather(place, [lambda z, y, x, core: gathered.at[z, y, x, core]], (), last_send, last_recv)
+    for stage in range(1, 6):
+        last.step(0, stage)
+    blocks = [gathered[n // 8, n // 4 % 2, n // 2 % 2, n % 2] for n in range(Z * Y * X * CORES)]
+    pos = jnp.concatenate([block[:, :D] for block in blocks[: ROWS // 8]], axis=0)
+    norm = jnp.concatenate([block[:, :D] for block in blocks[ROWS // 8 : ROWS // 8 + 2]], axis=0)
+    pos_sum[...] = jnp.concatenate([pos[NPATCH:TOK], pos[:NPATCH]], axis=0)
+    norm_sum[...] = norm[: 4 * L + 2]
+    total = blocks[0][:, D:]
+    for block in blocks[1:]:
+        total = total + block[:, D:]
+    rest = jnp.sum(pos * pos, axis=0, keepdims=True) + jnp.sum(norm * norm, axis=0, keepdims=True) + squares[1:2, :]
+    total = total[0:1, :] + jnp.sum(rest, axis=(0, 1), keepdims=True)
+    norm_all = jnp.sqrt(total)
+    stats[...] = jnp.concatenate(
+        [blocks[ROWS // 8 + 2][0:1, :128], norm_all, jnp.minimum(1.0, MAX_NORM / norm_all), jnp.zeros((5, 128), F32)],
+        axis=0,
     )
-    scratch = [((ALL, D), F32), ((ALL, D), F32), ((ALL, D), BF16), ((ALL, D), BF16), ((ALL, 3 * D), BF16)]
-    scratch += [((2,) + shape[1:], kind) for shape, kind in SAVED[1:9]]
+    scatter.finish()
+    heads.finish()
+    last.finish()
+
+
+def backward(sharded, *operands):
+    full = ((PATCH_SHAPE, BF16), (ATTN_SHAPE, BF16), (MLP_SHAPE, BF16))
+    if sharded:
+        outs = (
+            ((PATCH_DIM // (Z * Y * X * CORES), D), F32),
+            ((L, 48, D), F32),
+            ((L, 2, 48, D), F32),
+            ((2 * C, D), F32),
+            ((TOK, D), F32),
+            ((4 * L + 2, D), F32),
+            ((8, 128), F32),
+        )
+    else:
+        outs = full + (((16, D), F32), ((ROWS, D), F32))
+    scratch = [((ALL, D), F32), ((ALL, D), F32), ((ALL, D), BF16), ((ALL, D), BF16), ((ALL, 3 * D), BF16), SAVED[0]]
+    scratch = [pltpu.VMEM(*entry) for entry in scratch]
+    scratch += [pltpu.VMEM(shape[1:], kind) for shape, kind in SAVED[1:]]
+    scratch += [pltpu.SemaphoreType.DMA((11,))]
+    if sharded:
+        scratch += [pltpu.VMEM(*entry) for entry in full]
+        scratch += [
+            pltpu.VMEM(SMALL_SHAPE, F32),
+            pltpu.VMEM((16, D), F32),
+            pltpu.VMEM(SMALL_SHAPE, F32),
+            pltpu.VMEM((Z, Y, X, CORES, 8, 2 * C), F32),
+            pltpu.VMEM((Z * Y * X * CORES * 8, 2 * C), BF16),
+            pltpu.VMEM((Z, Y, X, CORES, 8, D + 128), F32),
+            pltpu.VMEM((8, D), F32),
+        ]
+        scratch += scatter_scratch()
+        scratch += [pltpu.SemaphoreType.DMA((N_GRADS, 8))] * 2
+        scratch += [pltpu.SemaphoreType.DMA((2, PIECES))] * 2 + [pltpu.SemaphoreType.DMA((1, PIECES))] * 2
+    params = dict(collective_id=1, has_side_effects=True) if sharded else {}
     return pl.pallas_call(
-        backward_kernel,
+        lambda *refs: backward_kernel(sharded, *refs),
         out_shape=[jax.ShapeDtypeStruct(*entry) for entry in outs],
-        in_specs=[VMEM] * 5 + [HBM] * 8,
+        in_specs=[VMEM] * 2 + [HBM] * 11 + [VMEM] * (4 if sharded else 0),
         out_specs=[VMEM] * len(outs),
-        scratch_shapes=[pltpu.VMEM(*entry) for entry in scratch] + [pltpu.SemaphoreType.DMA((2, 8))],
-        compiler_params=pltpu.CompilerParams(vmem_limit_bytes=62 * 2**20),
+        scratch_shapes=scratch,
+        compiler_params=pltpu.CompilerParams(vmem_limit_bytes=63 * 2**20, **params),
         name="backward",
     )(*operands)
 
@@ -653,30 +944,36 @@
         head_weight.T, norm_params, *weights_in,
     )
     saved, (loss, feature, dlogits, dtop, dnorm) = results[: len(SAVED)], results[len(SAVED) :]
-    features = lax.all_gather(feature.astype(BF16), axes, axis=0, tiled=True)
-    all_dlogits = lax.all_gather(dlogits.astype(BF16), axes, axis=0, tiled=True)
-    head_sum = tn(all_dlogits, features).T
-    grad_patch, grad_attn, grad_mlp, grad_norm, grad_pos = backward(
-        dtop, norm_params, saved[0], *saved[9:], *saved[1:9]
-    )
-    patch_share = lax.psum_scatter(grad_patch.astype(F32), axes, scatter_dimension=0, tiled=True)
-    attn_share = lax.psum_scatter(grad_attn.astype(F32), axes, scatter_dimension=1, tiled=True)
-    mlp_share = lax.psum_scatter(grad_mlp.astype(F32), "mp", scatter_dimension=2, tiled=True)
-    mlp_share = lax.psum_scatter(mlp_share, "dp", scatter_dimension=3, tiled=True)
+    operands = (dtop, norm_params, *saved)
+    if sharded:
+        patch_share, attn_share, mlp_share, head_sum, pos_sum, norm_sum, stats = backward(
+            True, *operands, loss, feature, dlogits, dnorm
+        )
+        loss_sum, global_norm, factor = stats[0, 0], stats[1, 0], stats[2, 0]
+        mlp_share = mlp_share.reshape(mlp_weight.shape)
+    else:
+        grad_patch, grad_attn, grad_mlp, grad_norm, grad_pos = backward(False, *operands)
+        rows = PATCH_DIM // (Z * Y * X * CORES)
+        grad_patch = grad_patch.reshape(-1, 32, D)[:, :rows].reshape(PATCH_DIM, D).astype(F32)
+        patch_share = lax.psum_scatter(grad_patch, axes, scatter_dimension=0, tiled=True)
+        grad_attn = grad_attn.reshape(L, 4 * D, D).astype(F32)
+        attn_share = lax.psum_scatter(grad_attn, axes, scatter_dimension=1, tiled=True)
+        grad_mlp = grad_mlp.reshape(L, 2, BLOCKS, D, D).astype(F32)
+        mlp_share = lax.psum_scatter(grad_mlp, "mp", scatter_dimension=2, tiled=True)
+        mlp_share = lax.psum_scatter(mlp_share, "dp", scatter_dimension=3, tiled=True)
+        mlp_share = mlp_share.reshape(mlp_weight.shape)
+        features = lax.all_gather(feature.astype(BF16), axes, axis=0, tiled=True)
+        all_dlogits = lax.all_gather(dlogits.astype(BF16), axes, axis=0, tiled=True)
+        head_sum = tn(all_dlogits, features)
+        grad_norms = jnp.concatenate([grad_norm[: 4 * L], dnorm[:2]], axis=0)
+        grad_pos = jnp.concatenate([grad_pos[NPATCH:TOK], grad_pos[:NPATCH]], axis=0)
+        pos_sum, norm_sum, loss_sum = lax.psum((grad_pos, grad_norms, loss[0, 0]), axes)
+        own_squares = sum(jnp.sum(share * share) for share in (patch_share, attn_share, mlp_share))
+        shared = sum(jnp.sum(total * total) for total in (pos_sum, head_sum, norm_sum))
+        global_norm = jnp.sqrt(lax.psum(own_squares, axes) + shared)
+        factor = jnp.minimum(1.0, MAX_NORM / global_norm)
     attn_share = jnp.swapaxes(attn_share, 1, 2)
-    mlp_share = mlp_share.reshape(mlp_weight.shape)
-    grad_norms = jnp.concatenate([grad_norm[: 4 * L], dnorm[:2]], axis=0)
-    pos_sum, norm_sum, loss_sum = lax.psum(
-        (jnp.concatenate([grad_pos[NPATCH:TOK], grad_pos[:NPATCH]], axis=0), grad_norms, loss[0, 0]), axes
-    )
-    own_squares = (
-        jnp.sum(patch_share * patch_share)
-        + jnp.sum(attn_share * attn_share)
-        + jnp.sum(mlp_share * mlp_share)
-    )
-    shared = jnp.sum(pos_sum * pos_sum) + jnp.sum(head_sum * head_sum) + jnp.sum(norm_sum * norm_sum)
-    global_norm = jnp.sqrt(lax.psum(own_squares, axes) + shared)
-    factor = jnp.minimum(1.0, MAX_NORM / global_norm)
+    head_sum = head_sum.T
     weights = (patch_weight, attn_weight, mlp_weight, positions, head_weight, norm_params)
     firsts = (patch_first, attn_first, mlp_first, pos_first, head_first, norm_first)
     seconds = (patch_second, attn_second, mlp_second, pos_second, head_second, norm_second)

time: 674 us -> 224 us (0.33)
  blocking collectives: 374 us -> 0 us
  waiting for transfers between devices: 110 us -> 0 us
  Pallas kernels: 131 us -> 198 us
  between operations: 19.8 us -> 0.99 us
  local copies, waits for them, and re-layouts: 10.6 us -> 1.4 us
    unnamed x1 -> x0, blocking collectives: 248 us -> none
    reduce_scatter x2 -> x0, waiting for transfers between devices: 110 us -> none  [the longest x1 110 us: per_device(): lax.psum_scatter(grad_attn.astype(F32), axes, scatter_dimension=1, tiled=...]
    all_gather x2 -> x0, blocking collectives: 84.1 us -> none  [the longest x1 42.5 us: per_device(): features = lax.all_gather(feature.astype(BF16), axes, axis=0, tiled=True)]
    pallas_call x1, Pallas kernels: 59.2 us -> 126 us  [backward(): pl.pallas_call(lambda *refs: backward_kernel(sharded, *refs), out_shape=[...]
    psum x1 -> x0, blocking collectives: 41.7 us -> none  [per_device(): lax.psum((jnp.concatenate([grad_pos[NPATCH:TOK], grad_pos[:NPATCH]], axis...]
    sub x6, other arithmetic: 11.5 us -> 20 us  [adam_update(): weight - step_rate * (adam_move + DECAY * weight)]
    reduce_sum x5 -> x0, other arithmetic: 6.98 us -> none  [the longest x1 1.74 us: per_device(): jnp.sum(mlp_share * mlp_share)]
    unnamed x50 -> x14, local copies, waits for them, and re-layouts: 6.99 us -> 0.04 us
  transfers between devices with their start and end apart: 4 -> 0, of which waited for: 1 -> 0; matrix products, arithmetic and copies ran while one was open for 3% -> 0% of each run, Pallas kernels for 0% -> 0%
where the time goes in v3:
time: 224 us; the launch traced here: 220 us
  Pallas kernels  198 us (88%)
  other arithmetic  20 us (9%)
    pallas_call x1, Pallas kernels, backward(): pl.pallas_call(lambda *refs: backward_kernel(sharded, *refs), out_shape=[...  126 us
    pallas_call x1, Pallas kernels, forward(): pl.pallas_call(lambda *refs: forward_kernel(image_count, sharded, *refs),...  71.6 us
    sub x6, other arithmetic, adam_update(): weight - step_rate * (adam_move + DECAY * weight)  20 us

profile of v3, /device:TPU:1, one launch (start us, length us, event | category | flops | bytes accessed | tf_op | source)
XLA Modules:
  0.0 220.1 jit_solution(10056346397383146389)
XLA Ops:
  0.7 71.6 %forward.1 = (bf16[624,768]{1,0:T(8,128)(2,1)}, f32[3,624,384]{2,1,0:T(8,128)}, bf16[3,624,384]{2,1,0:T(8,128)(2,1)}, bf16[3,624,1152]{2,1,0:T(8,128)(2,1)}, bf1...) custom-call(s32[3]{0:T(128)} %refs_0_.1, ...), custom_call_target="tpu_custom_call" | custom-call | tf_op jit(solution)/shard_map/forward/pallas_call | solution.py:596
  72.2 0.0 copy-start.4
  72.3 0.0 copy-start.3
  72.3 0.0 copy-start.6
  72.3 126.1 %backward.1 = (f32[24,384]{1,0:T(8,128)}, f32[3,48,384]{2,1,0:T(8,128)}, f32[3,2,48,384]{3,2,1,0:T(8,128)}, f32[2000,384]{1,0:T(8,128)}, f32[198,384]{1,0:T(8,12...) custom-call(f32[8,384]{1,0:T(8,128)} %get-tuple-element.43.refs_0_, f32[14,384]{1,0:T(8,128)} %refs_1_.3, ...), custom_call_target="tpu_custom_call" | custom-call | tf_op jit(solution)/shard_map/backward/pallas_call | solution.py:901
  198.4 0.0 copy-start.2
  198.4 0.0 copy-start.5
  198.4 1.4 fusion.16
  199.8 2.1 multiply_subtract_fusion.5
  201.9 2.1 multiply_subtract_fusion.4
  204.0 0.0 copy-done.4
  204.0 0.0 copy-start
  204.0 0.0 copy-start.1
  204.0 3.2 %multiply_subtract_fusion.3 = (f32[3,384,48]{1,2,0:T(8,128)}, f32[3,384,48]{1,2,0:T(8,128)}, f32[3,384,48]{1,2,0:T(8,128)}) fusion(f32[3,384,48]{1,2,0:T(8,128)S(1)} %copy-done.4, f32[3,48,384]{2,1,0:T(8,128)} %get-tuple-element.61, f32[]{:T(128)} %bitcast.4, f32[3,384,48]{1,2,0:T(8,128)} %param.35, f32[3,384,48]{1,2,0:T(8,128)} %param.41), kind=kLoop, calls=%fused_computation.17 | loop fusion | flops 884736 | bytes 1548292 | tf_op jit(solution)/shard_map/sub | solution.py:921
  207.2 0.0 copy-done.3
  207.2 2.8 %multiply_subtract_fusion.2 = (f32[198,384]{1,0:T(8,128)}, f32[198,384]{1,0:T(8,128)}, f32[198,384]{1,0:T(8,128)}) fusion(f32[198,384]{1,0:T(8,128)S(1)} %copy-done.3, f32[198,384]{1,0:T(8,128)} %get-tuple-element.63, f32[]{:T(128)} %bitcast.4, f32[198,384]{1,0:T(8,128)} %param.37, f32[198,384]{1,0:T(8,128)} %param.43), kind=kLoop, calls=%fused_computation.12 | loop fusion | flops 1216512 | bytes 2128900 | tf_op jit(solution)/shard_map/sub | solution.py:921
  210.1 0.0 copy-done.6
  210.1 0.0 copy-done.2
  210.1 0.0 copy-done.5
  210.1 2.9 %multiply_subtract_fusion.1 = (f32[3,2,48,384]{3,2,1,0:T(8,128)}, f32[3,2,48,384]{3,2,1,0:T(8,128)}, f32[3,2,48,384]{3,2,1,0:T(8,128)}) fusion(f32[3,2,48,384]{3,2,1,0:T(8,128)S(1)} %copy-done.2, f32[3,2,48,384]{3,2,1,0:T(8,128)} %get-tuple-element.62, f32[]{:T(128)} %bitcast.4, f32[3,2,48,384]{3,2,1,0:T(8,128)S(1)} %copy-done.5, ...), kind=kLoop, calls=%fused_computation.8 | loop fusion | flops 1769472 | bytes 3096580 | tf_op jit(solution)/shard_map/sub | solution.py:921
  213.0 0.0 copy-done
  213.0 0.0 copy-done.1
  213.0 6.9 %multiply_subtract_fusion = (f32[384,2000]{0,1:T(8,128)}, f32[384,2000]{0,1:T(8,128)}, f32[384,2000]{0,1:T(8,128)}) fusion(f32[384,2000]{0,1:T(8,128)S(1)} %copy-done, f32[2000,384]{1,0:T(8,128)} %get-tuple-element.64, f32[]{:T(128)} %bitcast.4, f32[384,2000]{0,1:T(8,128)S(1)} %copy-done.1, f32[384,2000]{0,1:T(8,128)} %param.44), kind=kLoop, calls=%fused_computation.4 | loop fusion | flops 12288000 | bytes 21504004 | tf_op jit(solution)/shard_map/sub | solution.py:921
Async XLA Ops:
  72.2 131.7 %copy-start.4 = (f32[3,384,48]{1,2,0:T(8,128)S(1)}, f32[3,384,48]{1,2,0:T(8,128)}, u32[]{:S(2)}) copy-start(f32[3,384,48]{1,2,0:T(8,128)} %param.29) | copy-start | bytes 663556
  72.3 135.0 %copy-start.3 = (f32[198,384]{1,0:T(8,128)S(1)}, f32[198,384]{1,0:T(8,128)}, u32[]{:S(2)}) copy-start(f32[198,384]{1,0:T(8,128)} %refs_5_.1) | copy-start | bytes 912388
  72.3 137.8 %copy-start.6 = (f32[3,2,48,384]{3,2,1,0:T(8,128)S(1)}, f32[3,2,48,384]{3,2,1,0:T(8,128)}, u32[]{:S(2)}) copy-start(f32[3,2,48,384]{3,2,1,0:T(8,128)} %param.42) | copy-start | bytes 1327108
  198.4 11.6 %copy-start.2 = (f32[3,2,48,384]{3,2,1,0:T(8,128)S(1)}, f32[3,2,48,384]{3,2,1,0:T(8,128)}, u32[]{:S(2)}) copy-start(f32[3,2,48,384]{3,2,1,0:T(8,128)} %refs_10_.1) | copy-start | bytes 1327108
  198.4 11.6 %copy-start.5 = (f32[3,2,48,384]{3,2,1,0:T(8,128)S(1)}, f32[3,2,48,384]{3,2,1,0:T(8,128)}, u32[]{:S(2)}) copy-start(f32[3,2,48,384]{3,2,1,0:T(8,128)} %param.36) | copy-start | bytes 1327108
  204.0 9.0 %copy-start = (f32[384,2000]{0,1:T(8,128)S(1)}, f32[384,2000]{0,1:T(8,128)}, u32[]{:S(2)}) copy-start(f32[384,2000]{0,1:T(8,128)} %param.32) | copy-start | bytes 9216004
  204.0 9.0 %copy-start.1 = (f32[384,2000]{0,1:T(8,128)S(1)}, f32[384,2000]{0,1:T(8,128)}, u32[]{:S(2)}) copy-start(f32[384,2000]{0,1:T(8,128)} %param.38) | copy-start | bytes 9216004
